TPU v7x, 32 devices: a whole 2x2x4 slice. The times are simulated.
32 devices in a mesh: dom: 8 (over y, x, core), grp: 4 (over z).
Axes of the slice: x: 2, y: 2, z: 4, core: 2. Of those that a mesh axis runs over, the one named last changes fastest.
Arguments:
- positions: float32 [3, 16384], P(None, ('dom', 'grp')), may hold values from -6 to 6
- mass: float32 [16384], P(('dom', 'grp')), may hold values from 0.05 to 0.2
- smooth: float32 [16384], P(('dom', 'grp')), may hold values from 1.5 to 3.5
- counts: int32 [64], P(('dom', 'grp')), may hold values from 128 to 256
- tasks: int32 [2, 128], P(None, ('dom', 'grp')), may hold values from 0 to 23, as said below
Outputs:
- density: float32 [16384], P(('dom', 'grp'))
- accel: float32 [3, 16384], P(None, ('dom', 'grp'))
Inputs may be any that keep to these rules, and one draw needn't show every extreme that they name: In every slab, for each b the slab's tasks whose receiving cell lies among slab cells b * 2 to (b + 1) * 2 - 1 number at most 12, and exactly 12 for one b; a cell may receive no task.
All inputs are finite; a program needn't handle non-finite values.
Results may differ from a plain program's by a relative error of at most 0.00017.
Values sent between devices are 32-bit elements; how exact they have to be, the bound alone decides.
A program may use at most 64 MiB of HBM per device.

v0:
```python
import math

import jax
import jax.numpy as jnp
from jax import lax
from jax.sharding import PartitionSpec as P

CELL = 256


def padded(block, sides, width):
    for axis, dim in sides:
        count = lax.axis_size(axis)
        forward = [(i, i + 1) for i in range(count - 1)]
        forward.append((count - 1, 0))
        backward = [(target, source) for source, target in forward]
        low = lax.ppermute(
            lax.slice_in_dim(block, block.shape[dim] - width, None, axis=dim), axis, forward
        )
        high = lax.ppermute(lax.slice_in_dim(block, 0, width, axis=dim), axis, backward)
        block = jnp.concatenate([low, block, high], axis=dim)
    return block


def tile_terms(recv, source):
    diff_x = recv[0][:, None] - source[0][None, :]
    diff_y = recv[1][:, None] - source[1][None, :]
    diff_z = recv[2][:, None] - source[2][None, :]
    radius = jnp.sqrt(diff_x * diff_x + diff_y * diff_y + diff_z * diff_z)
    length = recv[4][:, None]
    inside = jnp.maximum(1.0 - radius / length, 0.0)
    return (diff_x, diff_y, diff_z, radius, length, inside)


def density_tile(recv, source):
    diff_x, diff_y, diff_z, radius, length, inside = tile_terms(recv, source)
    weight = inside**4 * (1.0 + 4.0 * radius / length) * (21.0 / (2.0 * math.pi)) / length**3
    return jnp.sum(weight * source[3][None, :], axis=1)


def force_tile(recv, source, rho_recv, rho_source):
    diff_x, diff_y, diff_z, radius, length, inside = tile_terms(recv, source)
    coeff = source[3][None, :] * (1.0 / rho_recv[:, None] + 1.0 / rho_source[None, :])
    coeff = coeff * inside**3 * (105.0 / math.pi) / length**5
    return jnp.stack(
        [jnp.sum(coeff * diff_x, 1), jnp.sum(coeff * diff_y, 1), jnp.sum(coeff * diff_z, 1)], 0
    )


def ghost_density(slab_rho):
    return padded(slab_rho, (("dom", 0),), slab_rho.shape[0])


def local(positions, mass, smooth, counts, tasks):
    count_here = positions.shape[1]
    cells_dev = counts.shape[0]
    groups = lax.axis_size("grp")
    slab_len = groups * count_here
    slab_cells = groups * cells_dev
    member = lax.axis_index("grp")
    live = (
        (lax.broadcasted_iota(jnp.int32, (cells_dev, CELL), 1) < counts[:, None])
        .astype(jnp.float32)
        .reshape(count_here)
    )
    packed = jnp.concatenate([positions, (mass * live)[None], smooth[None]], 0)
    slab_pack = lax.all_gather(packed, "grp", axis=1, tiled=True)
    pool = padded(slab_pack, (("dom", 1),), slab_len)

    def fetch(cell_row):
        return lax.dynamic_slice_in_dim(pool, cell_row * CELL, CELL, 1)

    def dens(pair):
        return density_tile(fetch(slab_cells + pair[0]), fetch(pair[1]))

    own_start = member * count_here
    self_term = mass * (21.0 / (2.0 * math.pi)) / smooth**3
    recv_rows = tasks[0]
    source_rows = tasks[1]
    onehot = (recv_rows[:, None] == lax.broadcasted_iota(jnp.int32, (1, slab_cells), 1)).astype(
        jnp.float32
    )
    partial_value = lax.map(dens, (recv_rows, source_rows), batch_size=4)
    slab_part = jnp.einsum(
        "tk,tc->kc", onehot, partial_value, precision=lax.Precision.HIGHEST
    ).reshape(slab_len)
    own_part = lax.dynamic_slice_in_dim(slab_part, own_start, count_here, 0) + self_term
    slab_part = lax.dynamic_update_slice_in_dim(slab_part, own_part, own_start, 0)
    slab_rho = lax.psum(slab_part, "grp")
    own_rho = lax.dynamic_slice_in_dim(slab_rho, own_start, count_here, 0)
    pool_rho = ghost_density(slab_rho)

    def fetch_rho(cell_row):
        return lax.dynamic_slice_in_dim(pool_rho, cell_row * CELL, CELL, 0)

    def force(pair):
        recv_row = slab_cells + pair[0]
        return force_tile(fetch(recv_row), fetch(pair[1]), fetch_rho(recv_row), fetch_rho(pair[1]))

    force_part = lax.map(force, (recv_rows, source_rows), batch_size=4)
    slab_force = jnp.einsum(
        "tk,tdc->dkc", onehot, force_part, precision=lax.Precision.HIGHEST
    ).reshape(3, slab_len)
    accel = lax.psum_scatter(slab_force, "grp", scatter_dimension=1, tiled=True)
    return (own_rho * live, accel * live[None, :])


def solution(mesh):
    in_specs = (
        P(None, ("dom", "grp")),
        P(("dom", "grp")),
        P(("dom", "grp")),
        P(("dom", "grp")),
        P(None, ("dom", "grp")),
    )
    out_specs = (P(("dom", "grp")), P(None, ("dom", "grp")))
    return jax.shard_map(local, mesh=mesh, in_specs=in_specs, out_specs=out_specs, check_vma=False)
```

profile of v0, /device:TPU:0, one launch (start us, length us, event | category | flops | bytes accessed | tf_op | source)
XLA Modules:
  0.0 106.2 jit_solution(3055616844055682662)
XLA Ops:
  7.2 0.7 iota_compare_fusion.2
  8.7 14.9 %all_gather.3 = f32[5,2048]{1,0:T(8,128)S(1)} all-gather(f32[5,512]{1,0:T(8,128)S(1)} %pad_maximum_fusion), channel_id=1, replica_groups=mesh['dom'=8,'grp'=4] {'grp'}, dimensions={1}, use_global_device_ids=true | all-gather | bytes 51200 | tf_op jit(solution)/shard_map/all_gather | solution.py:67
  23.6 2.6 %collective-permute-start.1 = (f32[5,2048]{1,0:T(8,128)S(1)}, f32[5,2048]{1,0:T(8,128)S(1)}, u32[]{:S(2)}, u32[]{:S(2)}) collective-permute-start(f32[5,2048]{1,0:T(8,128)S(1)} %all_gather.3), channel_id=1, source_target_pairs={{4,0},{8,4},{12,8},{16,12},{20,16},{24,20},{28,24},{0,28},{5,1},{9... | collective-permute-start | bytes 122888 | tf_op jit(solution)/shard_map/ppermute | solution.py:20
  26.3 1.9 %collective-permute-done = f32[5,2048]{1,0:T(8,128)S(1)} collective-permute-done((f32[5,2048]{1,0:T(8,128)S(1)}, f32[5,2048]{1,0:T(8,128)S(1)}, u32[]{:S(2)}, u32[]{:S(2)}) %collective-permute-start) | collective-permute-done | bytes 40992 | tf_op jit(solution)/shard_map/ppermute | solution.py:17
  28.2 5.8 %while.5 = (s32[]{:T(128)}, f32[5,6144]{1,0:T(8,128)S(1)}, s32[4,2]{0,1:T(2,128)S(1)}, f32[4,5,256]{2,1,0:T(8,128)S(1)}, s32[]{:T(128)}) while((s32[]{:T(128)}, f32[5,6144]{1,0:T(8,128)S(1)}, s32[4,2]{0,1:T(2,128)S(1)}, f32[4,5,256]{2,1,0:T(8,128)S(1)}, s32[]{:T(128)}) %tuple.71), condition=%wide.while_cond.1, body=%wide.while_body.1.sunk | while | flops 2 | bytes 16489 | solution.py:71
  28.9 0.8 bitcast_dynamic-update-slice_fusion.5
  30.4 0.8 bitcast_dynamic-update-slice_fusion.5
  31.8 0.8 bitcast_dynamic-update-slice_fusion.5
  33.2 0.8 bitcast_dynamic-update-slice_fusion.5
  34.0 5.3 %while.4 = (s32[]{:T(128)}, f32[5,6144]{1,0:T(8,128)S(1)}, s32[4,2]{0,1:T(2,128)S(1)}, f32[4,5,256]{2,1,0:T(8,128)S(1)}, s32[]{:T(128)}) while((s32[]{:T(128)}, f32[5,6144]{1,0:T(8,128)S(1)}, s32[4,2]{0,1:T(2,128)S(1)}, f32[4,5,256]{2,1,0:T(8,128)S(1)}, s32[]{:T(128)}) %tuple.85), condition=%wide.while_cond, body=%wide.while_body.sunk | while | flops 2 | bytes 16489 | solution.py:71
  39.4 1.3 %fusion.13 = f32[4,256]{1,0:T(4,128)S(1)} fusion(f32[4,256]{1,0:T(4,128)S(1)} %get-tuple-element.114, f32[4,256]{1,0:T(4,128)S(1)} %get-tuple-element.111, f32[4,256]{1,0:T(4,128)S(1)} %get-tuple-element.118, f32[4,256]{1,0:T(4,128)S(1)} %get-tuple-element.115, f32[4,256]{1,0:T(4,128)S(1)} %get-tuple-element.119, f32[4,256]{1,0:T(4,128)S(1)} %get-tuple-element.116, ...), kind=kLoop, calls=%fused_computation.30 | loop fusion | flops 5504000 | bytes 40960 | tf_op jit(solution)/shard_map/while/body/eval_jaxpr/vmap()/reduce_sum | solution.py:38
  41.1 11.9 %psum.7 = f32[2048]{0:T(1024)S(1)} all-reduce(f32[2048]{0:T(1024)S(1)} %fusion.21), channel_id=1, replica_groups=mesh['dom'=8,'grp'=4] {'grp'}, use_global_device_ids=true, to_apply=%region_1.0 | all-reduce | flops 2048 | bytes 16384 | tf_op jit(solution)/shard_map/psum | solution.py:89
  53.2 2.6 %collective-permute-start.3 = (f32[2048]{0:T(1024)S(1)}, f32[2048]{0:T(1024)S(1)}, u32[]{:S(2)}, u32[]{:S(2)}) collective-permute-start(f32[2048]{0:T(1024)S(1)} %psum.7), channel_id=1, source_target_pairs={{4,0},{8,4},{12,8},{16,12},{20,16},{24,20},{28,24},{0,28},{5,1},{9... | collective-permute-start | bytes 24584 | tf_op jit(solution)/shard_map/ppermute | solution.py:20
  55.8 1.3 %collective-permute-done.2 = f32[2048]{0:T(1024)S(1)} collective-permute-done((f32[2048]{0:T(1024)S(1)}, f32[2048]{0:T(1024)S(1)}, u32[]{:S(2)}, u32[]{:S(2)}) %collective-permute-start.2) | collective-permute-done | bytes 8224 | tf_op jit(solution)/shard_map/ppermute | solution.py:17
  57.2 5.9 %while.7 = (s32[]{:T(128)}, f32[6144]{0:T(1024)S(1)}, s32[4,1]{0,1:T(1,128)S(1)}, f32[4,256]{1,0:T(4,128)S(1)}, s32[]{:T(128)}, /*index=5*/s32[]{:T(128)}) while((s32[]{:T(128)}, f32[6144]{0:T(1024)S(1)}, s32[4,1]{0,1:T(1,128)S(1)}, f32[4,256]{1,0:T(4,128)S(1)}, s32[]{:T(128)}, /*index=5*/s32[]{:T(128)}) %tuple.77), condition=%wide.while_cond.3, body=%wide.while_body.3.sunk | while | flops 2 | bytes 4193 | solution.py:94
  57.8 0.8 dynamic-slice.35
  59.3 0.8 dynamic-slice.35
  60.8 0.8 dynamic-slice.35
  62.2 0.8 dynamic-slice.35
  63.0 5.4 %while.6 = (s32[]{:T(128)}, f32[6144]{0:T(1024)S(1)}, s32[4,1]{0,1:T(1,128)S(1)}, f32[4,256]{1,0:T(4,128)S(1)}, s32[]{:T(128)}, /*index=5*/s32[]{:T(128)}) while((s32[]{:T(128)}, f32[6144]{0:T(1024)S(1)}, s32[4,1]{0,1:T(1,128)S(1)}, f32[4,256]{1,0:T(4,128)S(1)}, s32[]{:T(128)}, /*index=5*/s32[]{:T(128)}) %tuple.86), condition=%wide.while_cond.2, body=%wide.while_body.2.sunk | while | flops 2 | bytes 4193 | solution.py:94
  68.4 1.8 %fusion.3 = (f32[4,256]{1,0:T(4,128)S(1)}, f32[4,256]{1,0:T(4,128)S(1)}, f32[4,256]{1,0:T(4,128)S(1)}) fusion(f32[4,256]{1,0:T(4,128)S(1)} %get-tuple-element.117, f32[4,256]{1,0:T(4,128)S(1)} %get-tuple-element.121, f32[4,256]{1,0:T(4,128)S(1)} %get-tuple-element.110, f32[4,256]{1,0:T(4,128)S(1)} %get-tuple-element.118, ...), kind=kLoop, calls=%fused_computation.19 | loop fusion | flops 6288384 | bytes 57344 | tf_op jit(solution)/shard_map/while/body/eval_jaxpr/vmap()/reduce_sum | solution.py:46
  70.5 1.4 %copy.9 = f32[3,8,256]{0,2,1:T(8,128)} copy(f32[3,8,256]{2,1,0:T(8,128)S(1)} %convolution_bitcast_fusion) | data formatting | bytes 49152
  72.6 25.1 %reduce-scatter.4.cloned.1.call-done = f32[512,3]{1,0:T(8,128)} async-done(((f32[2048,3]{1,0:T(8,128)}), f32[512,3]{1,0:T(8,128)}) %reduce-scatter.4.cloned.1.call-update) | async-done | bytes 6160
  97.7 1.1 copy.8
  (87 shorter events, 19.0 us)
Async XLA Ops:
  7.2 0.8 copy-start.2
  7.2 0.8 copy-start.1
  7.2 90.5 %reduce-scatter.4.cloned.1.call-start = ((), (), s32[]{:S(2)}) async-start(), calls=%async_computation.1 | async-start | bytes 1310720
  8.0 0.7 copy-start
  8.7 17.6 %copy-start.3 = (s32[2,4]{1,0:T(2,128)S(1)}, s32[2,4]{1,0:T(2,128)}, u32[]{:S(2)}) copy-start(s32[2,4]{1,0:T(2,128)} %param.9) | copy-start | bytes 100
  23.6 4.6 %collective-permute-start = (f32[5,2048]{1,0:T(8,128)S(1)}, f32[5,2048]{1,0:T(8,128)S(1)}, u32[]{:S(2)}, u32[]{:S(2)}) collective-permute-start(f32[5,2048]{1,0:T(8,128)S(1)} %all_gather.3), channel_id=1, source_target_pairs={{0,4},{4,8},{8,12},{12,16},{16,20},{20,24},{24,28},{28,0},{1,5},{5... | collective-permute-start | bytes 122888 | tf_op jit(solution)/shard_map/ppermute | solution.py:17
  23.6 4.6 %collective-permute-start.1 = (f32[5,2048]{1,0:T(8,128)S(1)}, f32[5,2048]{1,0:T(8,128)S(1)}, u32[]{:S(2)}, u32[]{:S(2)}) collective-permute-start(f32[5,2048]{1,0:T(8,128)S(1)} %all_gather.3), channel_id=1, source_target_pairs={{4,0},{8,4},{12,8},{16,12},{20,16},{24,20},{28,24},{0,28},{5,1},{9... | collective-permute-start | bytes 122888 | tf_op jit(solution)/shard_map/ppermute | solution.py:20
  53.1 4.0 %collective-permute-start.2 = (f32[2048]{0:T(1024)S(1)}, f32[2048]{0:T(1024)S(1)}, u32[]{:S(2)}, u32[]{:S(2)}) collective-permute-start(f32[2048]{0:T(1024)S(1)} %psum.7), channel_id=1, source_target_pairs={{0,4},{4,8},{8,12},{12,16},{16,20},{20,24},{24,28},{28,0},{1,5},{5... | collective-permute-start | bytes 24584 | tf_op jit(solution)/shard_map/ppermute | solution.py:17
  53.2 4.0 %collective-permute-start.3 = (f32[2048]{0:T(1024)S(1)}, f32[2048]{0:T(1024)S(1)}, u32[]{:S(2)}, u32[]{:S(2)}) collective-permute-start(f32[2048]{0:T(1024)S(1)} %psum.7), channel_id=1, source_target_pairs={{4,0},{8,4},{12,8},{16,12},{20,16},{24,20},{28,24},{0,28},{5,1},{9... | collective-permute-start | bytes 24584 | tf_op jit(solution)/shard_map/ppermute | solution.py:20
Sparse Core Ops, SparseCore 0:
  72.0 25.5 reduce-scatter.3
where the time goes:
time: 107 us; the launch traced here: 106 us
  waiting for transfers between devices  28.4 us (27%)
  blocking collectives  26.8 us (25%)
  local copies, waits for them, and re-layouts  25.4 us (24%)
  between operations  14.2 us (13%)
  starting transfers between devices  5.36 us (5%)
  other arithmetic  5.35 us (5%)
    unnamed x2, waiting for transfers between devices  25.1 us
    gather x48, local copies, waits for them, and re-layouts  22.2 us
    all_gather x1, blocking collectives, local(): slab_pack = lax.all_gather(packed, 'grp', axis=1, tiled=True)  14.9 us
    psum x1, blocking collectives, local(): slab_rho = lax.psum(slab_part, 'grp')  11.9 us
    ppermute x2, starting transfers between devices, padded(): lax.ppermute(lax.slice_in_dim(block, 0, width, axis=dim), axis, backward)  5.27 us
    ppermute x2, waiting for transfers between devices, padded(): lax.ppermute(lax.slice_in_dim(block, block.shape[dim] - width, None, axis...  3.21 us
    unnamed x23, local copies, waits for them, and re-layouts  3.15 us
  transfers between devices with their start and end apart: 5, of which 3 were waited for; matrix products, arithmetic and copies ran while one was open for 1% of the time, Pallas kernels for 0%

commit v1 on v0

v1 whole, which is shorter than its diff:
```python
import functools
import math

import jax
import jax.numpy as jnp
from jax import lax
from jax.experimental import pallas as pl
from jax.experimental.pallas import tpu as pltpu
from jax.sharding import PartitionSpec as P

CELL = 256
LANES = 128
HALVES = CELL // LANES
CHUNK = 32
MESH = pl.DeviceIdType.MESH
DENSITY_SCALE = 21.0 / (2.0 * math.pi)
FORCE_SCALE = 105.0 / math.pi


def kernel(
    doms, groups, pairs, tasks_ref, counts_ref, pos_ref, mass_ref, smooth_ref,
    rho_out, acc_out,
    pool, parts, rho, tasks_v, tasks_s, send_sem, recv_sem, psend_sem, precv_sem, tsend_sem, trecv_sem, local_sem,
):
    cells = counts_ref.shape[0]
    slab_cells = groups * cells
    dom = lax.axis_index("dom")
    member = lax.axis_index("grp")
    own = groups + member
    peers = [(e, g) for e in (0, -1, 1) for g in range(groups) if not (e == 0 and g == 0)]

    def place(e, g):
        return (lax.rem(dom + e + doms, doms), lax.rem(member + g, groups))

    barrier = pltpu.get_barrier_semaphore()
    for e, g in peers:
        pl.semaphore_signal(barrier, inc=1, device_id=place(e, g), device_id_type=MESH)

    lane = lax.broadcasted_iota(jnp.int32, (1, LANES), 1)
    for c in range(cells):
        for h in range(HALVES):
            at = pl.ds(c * CELL + h * LANES, LANES)
            live = (lane + h * LANES < counts_ref[c]).astype(jnp.float32)
            for d in range(3):
                pool[own, c, pl.ds(d * HALVES + h, 1), :] = pos_ref[pl.ds(d, 1), at]
            pool[own, c, pl.ds(3 * HALVES + h, 1), :] = mass_ref[:, at] * live
            pool[own, cells, pl.ds(c * HALVES + h, 1), :] = smooth_ref[:, at]
    row = jnp.zeros((1, LANES), jnp.int32)
    for t in range(pairs):
        pool[own, cells, pl.ds(cells * HALVES + t, 1), :] = jnp.full((1, LANES), tasks_ref[0, t]).astype(jnp.float32)
        row = jnp.where(lane == t, tasks_ref[0, t], row)
        row = jnp.where(lane == pairs + t, tasks_ref[1, t], row)
    tasks_v[member] = row

    def exchange(ref, sends, recvs, e, g, n):
        slot = (1 - e) * groups + member
        return pltpu.make_async_remote_copy(
            src_ref=ref.at[own], dst_ref=ref.at[slot], send_sem=sends.at[n], recv_sem=recvs.at[slot],
            device_id=place(e, g), device_id_type=MESH,
        )

    def arrival(ref, sends, recvs, e, g):
        slot = (1 + e) * groups + lax.rem(member + g, groups)
        return pltpu.make_async_remote_copy(
            src_ref=ref.at[own], dst_ref=ref.at[slot], send_sem=sends.at[0], recv_sem=recvs.at[slot],
            device_id=place(e, g), device_id_type=MESH,
        )

    pl.semaphore_wait(barrier, len(peers))
    first = [exchange(pool, send_sem, recv_sem, e, g, n) for n, (e, g) in enumerate(peers)]
    for copy in first:
        copy.start()
    lists = []
    for g in range(1, groups):
        copy = pltpu.make_async_remote_copy(
            src_ref=tasks_v.at[member], dst_ref=tasks_v.at[member], send_sem=tsend_sem.at[g],
            recv_sem=trecv_sem.at[member], device_id=place(0, g), device_id_type=MESH,
        )
        copy.start()
        lists.append(copy)
    for g in range(1, groups):
        other = lax.rem(member + g, groups)
        pltpu.make_async_remote_copy(
            src_ref=tasks_v.at[member], dst_ref=tasks_v.at[other], send_sem=tsend_sem.at[0],
            recv_sem=trecv_sem.at[other], device_id=place(0, g), device_id_type=MESH,
        ).wait_recv()
    to_scalar = pltpu.make_async_copy(tasks_v, tasks_s, local_sem)
    to_scalar.start()
    for e, g in peers:
        arrival(pool, send_sem, recv_sem, e, g).wait_recv()

    def receiver(slot, cell):
        block = pool[slot, cell]
        rest = pool[slot, cells]
        length = rest[0:HALVES]
        for c in range(1, cells):
            length = jnp.where(cell == c, rest[c * HALVES:(c + 1) * HALVES], length)
        inverse = 1.0 / length
        rows = []
        for h in range(HALVES):
            rows.append([block[d * HALVES + h:d * HALVES + h + 1] for d in range(3)] + [inverse[h:h + 1]])
        return rows

    def chunks(source):
        for s in range(HALVES):
            for q in range(0, LANES, CHUNK):
                yield s, q, [source[q:q + CHUNK, d * HALVES + s:d * HALVES + s + 1] for d in range(4)]

    def inside(row, col):
        diffs = [row[d] - col[d] for d in range(3)]
        square = (diffs[0] * diffs[0] + diffs[1] * diffs[1] + diffs[2] * diffs[2]) * (row[3] * row[3])
        ratio = square * lax.rsqrt(jnp.maximum(square, 1e-30))
        return diffs, jnp.maximum(1.0 - ratio, 0.0)

    def density(t, carry):
        recv, k = tasks_ref[0, t], tasks_ref[1, t]
        rows = receiver(groups + recv // cells, lax.rem(recv, cells))
        source = jnp.transpose(pool[k // cells, lax.rem(k, cells)])
        total = [jnp.zeros((CHUNK, LANES), jnp.float32) for _ in range(HALVES)]
        for s, q, col in chunks(source):
            for h in range(HALVES):
                _, u = inside(rows[h], col)
                u2 = u * u
                total[h] = total[h] + (u2 * u2) * (5.0 - 4.0 * u) * col[3]
        for h in range(HALVES):
            value = jnp.sum(total[h], axis=0, keepdims=True)
            inv = rows[h][3]
            parts[own, pl.ds(t * HALVES + h, 1), :] = value * (inv * inv * inv) * DENSITY_SCALE
        return carry

    lax.fori_loop(0, pairs, density, 0)
    second = [exchange(parts, psend_sem, precv_sem, e, g, n) for n, (e, g) in enumerate(peers)]
    for copy in second:
        copy.start()

    for slot in range(3 * groups):
        for c in range(cells):
            m = pool[slot, c, pl.ds(3 * HALVES, HALVES), :]
            inv = 1.0 / pool[slot, cells, pl.ds(c * HALVES, HALVES), :]
            rho[pl.ds((slot * cells + c) * HALVES, HALVES), :] = m * (inv * inv * inv) * DENSITY_SCALE
    to_scalar.wait()

    for e, g in peers:
        arrival(parts, psend_sem, precv_sem, e, g).wait_recv()

    span = slab_cells * HALVES
    index = lax.broadcasted_iota(jnp.int32, (span, LANES), 0)
    odd = lax.rem(index, HALVES)
    cell_of = (index // HALVES).astype(jnp.float32)
    for d in range(3):
        total = rho[pl.ds(d * span, span), :]
        for g in range(groups):
            slot = d * groups + g
            part = parts[slot]
            to = pool[slot, cells]
            for t in range(pairs):
                value = part[t * HALVES:t * HALVES + 1]
                for h in range(1, HALVES):
                    value = jnp.where(odd == h, part[t * HALVES + h:t * HALVES + h + 1], value)
                at = to[cells * HALVES + t:cells * HALVES + t + 1]
                total = total + jnp.where(cell_of == at, value, 0.0)
        rho[pl.ds(d * span, span), :] = total

    for c in range(cells):
        for h in range(HALVES):
            rho_out[pl.ds(c * HALVES + h, 1), :] = rho[pl.ds((own * cells + c) * HALVES + h, 1), :]
    acc_out[...] = jnp.zeros_like(acc_out)

    def force(t, carry):
        j, i = t // pairs, lax.rem(t, pairs)
        recv, k = tasks_s[j, 0, i], tasks_s[j, 0, pairs + i]
        cell = lax.rem(recv, cells)
        mine = recv // cells == member
        rows = receiver(own, cell)
        block = pool[k // cells, lax.rem(k, cells)]
        k_rho = rho[pl.ds(k * HALVES, HALVES), :]
        weight = block[3 * HALVES:4 * HALVES] / jnp.maximum(k_rho, 1e-30)
        source = jnp.transpose(block)
        heavy = jnp.transpose(jnp.concatenate([weight] * (8 // HALVES), axis=0))
        a_rho = 1.0 / jnp.maximum(rho[pl.ds((own * cells + cell) * HALVES, HALVES), :], 1e-30)
        total = [[jnp.zeros((CHUNK, LANES), jnp.float32) for _ in range(3)] for _ in range(HALVES)]
        for s, q, col in chunks(source):
            ratio = heavy[q:q + CHUNK, s:s + 1]
            for h in range(HALVES):
                diffs, u = inside(rows[h], col)
                coeff = (u * u) * u * (col[3] * a_rho[h:h + 1] + ratio)
                for d in range(3):
                    total[h][d] = total[h][d] + coeff * diffs[d]
        for h in range(HALVES):
            inv = rows[h][3]
            fifth = FORCE_SCALE * (inv * inv) * (inv * inv) * inv
            for d in range(3):
                value = jnp.sum(total[h][d], axis=0, keepdims=True) * fifth
                for c in range(cells):
                    at = pl.ds((d * cells + c) * HALVES + h, 1)
                    acc_out[at, :] += jnp.where(jnp.logical_and(mine, cell == c), value, 0.0)
        return carry

    lax.fori_loop(0, groups * pairs, force, 0)
    for c in range(cells):
        for h in range(HALVES):
            live = (lane + h * LANES < counts_ref[c]).astype(jnp.float32)
            at = pl.ds(c * HALVES + h, 1)
            rho_out[at, :] = rho_out[at, :] * live
            for d in range(3):
                at = pl.ds((d * cells + c) * HALVES + h, 1)
                acc_out[at, :] = acc_out[at, :] * live

    for copy in first + lists + second:
        copy.wait_send()


def local(positions, mass, smooth, counts, tasks):
    groups, doms = lax.axis_size("grp"), lax.axis_size("dom")
    cells, pairs = counts.shape[0], tasks.shape[1]
    around = 3 * groups
    last = max(8, -(-(cells * HALVES + pairs) // 8) * 8)
    vmem, smem = (pl.BlockSpec(memory_space=space) for space in (pltpu.VMEM, pltpu.SMEM))
    density, accel = pl.pallas_call(
        functools.partial(kernel, doms, groups, pairs),
        out_shape=(
            jax.ShapeDtypeStruct((cells * HALVES, LANES), jnp.float32),
            jax.ShapeDtypeStruct((3 * cells * HALVES, LANES), jnp.float32),
        ),
        in_specs=[smem, smem, vmem, vmem, vmem],
        out_specs=(vmem, vmem),
        scratch_shapes=[
            pltpu.VMEM((around, cells + 1, last, LANES), jnp.float32),
            pltpu.VMEM((around, pairs * HALVES, LANES), jnp.float32),
            pltpu.VMEM((around * cells * HALVES, LANES), jnp.float32),
            pltpu.VMEM((groups, 1, LANES), jnp.int32),
            pltpu.SMEM((groups, 1, LANES), jnp.int32),
            pltpu.SemaphoreType.DMA((around,)),
            pltpu.SemaphoreType.DMA((around,)),
            pltpu.SemaphoreType.DMA((around,)),
            pltpu.SemaphoreType.DMA((around,)),
            pltpu.SemaphoreType.DMA((groups,)),
            pltpu.SemaphoreType.DMA((groups,)),
            pltpu.SemaphoreType.DMA,
        ],
        compiler_params=pltpu.CompilerParams(
            collective_id=0, has_side_effects=True, vmem_limit_bytes=48 * 1024 * 1024
        ),
    )(tasks, counts, positions, mass[None], smooth[None])
    return density.reshape(-1), accel.reshape(3, -1)


def solution(mesh):
    in_specs = (
        P(None, ("dom", "grp")),
        P(("dom", "grp")),
        P(("dom", "grp")),
        P(("dom", "grp")),
        P(None, ("dom", "grp")),
    )
    out_specs = (P(("dom", "grp")), P(None, ("dom", "grp")))
    return jax.shard_map(local, mesh=mesh, in_specs=in_specs, out_specs=out_specs, check_vma=False)
```

time: 107 us -> 30.1 us (0.28)
  waiting for transfers between devices: 28.4 us -> 0 us
  blocking collectives: 26.8 us -> 0 us
  Pallas kernels: 0 us -> 25.9 us
  local copies, waits for them, and re-layouts: 25.4 us -> 3.24 us
  between operations: 14.2 us -> 0.67 us
  starting transfers between devices: 5.36 us -> 0 us
  other arithmetic: 5.35 us -> 0 us
    pallas_call x0 -> x1, Pallas kernels: none -> 25.9 us  [local(): pl.pallas_call(functools.partial(kernel, doms, groups, pairs), out_shape=...]
    unnamed x2 -> x0, waiting for transfers between devices: 25.1 us -> none
    gather x48 -> x0, local copies, waits for them, and re-layouts: 22.2 us -> none
    all_gather x1 -> x0, blocking collectives: 14.9 us -> none  [local(): slab_pack = lax.all_gather(packed, 'grp', axis=1, tiled=True)]
    psum x1 -> x0, blocking collectives: 11.9 us -> none  [local(): slab_rho = lax.psum(slab_part, 'grp')]
    ppermute x4 -> x0, starting transfers between devices: 5.33 us -> none  [the longest x2 5.27 us: padded(): lax.ppermute(lax.slice_in_dim(block, 0, width, axis=dim), axis, backward)]
    ppermute x4 -> x0, waiting for transfers between devices: 3.25 us -> none  [the longest x2 3.21 us: padded(): lax.ppermute(lax.slice_in_dim(block, block.shape[dim] - width, None, axis...]
    reduce_sum x2 -> x0, other arithmetic: 3.11 us -> none  [the longest x1 1.81 us: force_tile(): jnp.sum(coeff * diff_x, 1)]
  transfers between devices with their start and end apart: 5 -> 0, of which waited for: 3 -> 0; matrix products, arithmetic and copies ran while one was open for 1% -> 0% of each run, Pallas kernels for 0% -> 0%
where the time goes in v1:
time: 30.1 us; the launch traced here: 29.8 us
  Pallas kernels  25.9 us (86%)
  local copies, waits for them, and re-layouts  3.24 us (11%)
  between operations  0.67 us (2%)
    pallas_call x1, Pallas kernels, local(): pl.pallas_call(functools.partial(kernel, doms, groups, pairs), out_shape=...  25.9 us
    unnamed x11, local copies, waits for them, and re-layouts  2.63 us
    reshape x1, local copies, waits for them, and re-layouts, local(): return (density.reshape(-1), accel.reshape(3, -1))  0.61 us

profile of v1, /device:TPU:0, one launch (start us, length us, event | category | flops | bytes accessed | tf_op | source)
XLA Modules:
  0.0 29.8 jit_solution(16146490543165506288)
XLA Ops:
  0.6 0.0 copy-start.1
  0.6 0.0 copy-start.3
  0.7 0.0 copy-start.4
  0.7 0.7 %copy-done.1 = f32[512]{0:T(512)S(1)} copy-done((f32[512]{0:T(512)S(1)}, f32[512]{0:T(512)}, u32[]{:S(2)}) %copy-start.1) | copy-done | bytes 2072
  1.3 0.0 copy-done.3
  1.3 0.0 copy-done.4
  1.3 0.0 copy-start
  1.3 0.7 %copy-done = f32[3,512]{1,0:T(4,128)S(1)} copy-done((f32[3,512]{1,0:T(4,128)S(1)}, f32[3,512]{1,0:T(4,128)}, u32[]{:S(2)}) %copy-start) | copy-done | bytes 6168
  2.0 0.0 copy-start.2
  2.0 0.7 %copy-done.2 = f32[512]{0:T(512)S(1)} copy-done((f32[512]{0:T(512)S(1)}, f32[512]{0:T(512)}, u32[]{:S(2)}) %copy-start.2) | copy-done | bytes 2072
  2.7 25.9 %shard_map.68 = (f32[4,128]{1,0:T(4,128)S(1)}, f32[12,128]{1,0:T(8,128)S(1)}) custom-call(s32[2,4]{1,0:T(2,128)S(1)} %copy-done.3, s32[2]{0:T(128)S(1)} %copy-done.4, f32[3,512]{1,0:T(4,128)S(1)} %copy-done, f32[1,512]{1,0:T(1,128)S(1)} %bitcast.3, f32[1,512]{1,0:T(1,128)S(1)} %bitcast.4), custom_call_target="tpu_custom_call" | custom-call | tf_op jit(solution)/shard_map/pallas_call | solution.py:219
  28.6 0.6 %reshape.11 = f32[3,512]{1,0:T(4,128)} reshape(f32[12,128]{1,0:T(8,128)S(1)} %get-tuple-element.5) | data formatting | bytes 12288 | tf_op jit(solution)/shard_map/reshape | solution.py:245
  29.2 0.6 %copy.8 = f32[512]{0:T(512)} copy(f32[512]{0:T(512)S(1)} %bitcast.5) | data formatting | bytes 4096
Async XLA Ops:
  0.6 0.7 %copy-start.1 = (f32[512]{0:T(512)S(1)}, f32[512]{0:T(512)}, u32[]{:S(2)}) copy-start(f32[512]{0:T(512)} %param.6) | copy-start | bytes 6148
  0.6 0.7 %copy-start.3 = (s32[2,4]{1,0:T(2,128)S(1)}, s32[2,4]{1,0:T(2,128)}, u32[]{:S(2)}) copy-start(s32[2,4]{1,0:T(2,128)} %tasks_ref.1) | copy-start | bytes 100
  0.7 0.7 %copy-start.4 = (s32[2]{0:T(128)S(1)}, s32[2]{0:T(128)}, u32[]{:S(2)}) copy-start(s32[2]{0:T(128)} %counts_ref.1) | copy-start | bytes 28
  1.3 0.7 %copy-start = (f32[3,512]{1,0:T(4,128)S(1)}, f32[3,512]{1,0:T(4,128)}, u32[]{:S(2)}) copy-start(f32[3,512]{1,0:T(4,128)} %pos_ref.1) | copy-start | bytes 18436
  2.0 0.7 %copy-start.2 = (f32[512]{0:T(512)S(1)}, f32[512]{0:T(512)}, u32[]{:S(2)}) copy-start(f32[512]{0:T(512)} %param.7) | copy-start | bytes 6148

commit v2 on v1

v2 whole, which is shorter than its diff:
```python
import functools
import math

import jax
import jax.numpy as jnp
from jax import lax
from jax.experimental import pallas as pl
from jax.experimental.pallas import tpu as pltpu
from jax.sharding import PartitionSpec as P

CELL = 256
LANES = 128
HALVES = CELL // LANES
CHUNK = 32
MESH = pl.DeviceIdType.MESH
DENSITY_SCALE = 21.0 / (2.0 * math.pi)
FORCE_SCALE = 105.0 / math.pi


def kernel(
    doms, groups, cells, pairs, tasks_hbm, counts_hbm, pos_hbm, mass_hbm, smooth_hbm,
    rho_out, acc_out,
    tasks_ref, counts_ref, pos_ref, mass_ref, smooth_ref,
    pool, parts, rho, forces, waiting, early,
    in_sem, send_sem, recv_sem, psend_sem, precv_sem, fsend_sem, frecv_sem,
):
    slab_cells = groups * cells
    dom = lax.axis_index("dom")
    member = lax.axis_index("grp")
    own = groups + member
    peers = [(e, g) for e in (0, -1, 1) for g in range(groups) if not (e == 0 and g == 0)]

    def place(e, g):
        return (lax.rem(dom + e + doms, doms), lax.rem(member + g, groups))

    barrier = pltpu.get_barrier_semaphore()
    for e, g in peers:
        pl.semaphore_signal(barrier, inc=1, device_id=place(e, g), device_id_type=MESH)
    moves = (
        (tasks_hbm, tasks_ref), (counts_hbm, counts_ref), (pos_hbm, pos_ref), (mass_hbm, mass_ref),
        (smooth_hbm, smooth_ref),
    )
    inputs = [pltpu.make_async_copy(*move, in_sem.at[n]) for n, move in enumerate(moves)]
    for copy in inputs:
        copy.start()
    for copy in inputs:
        copy.wait()

    lane = lax.broadcasted_iota(jnp.int32, (1, LANES), 1)
    for c in range(cells):
        for h in range(HALVES):
            at = pl.ds(c * CELL + h * LANES, LANES)
            live = (lane + h * LANES < counts_ref[c]).astype(jnp.float32)
            for d in range(3):
                pool[own, c, pl.ds(d * HALVES + h, 1), :] = pos_ref[pl.ds(d, 1), at]
            pool[own, c, pl.ds(3 * HALVES + h, 1), :] = mass_ref[:, at] * live
            pool[own, cells, pl.ds(c * HALVES + h, 1), :] = smooth_ref[:, at]
    for t in range(pairs):
        pool[own, cells, pl.ds(cells * HALVES + t, 1), :] = jnp.full((1, LANES), tasks_ref[0, t]).astype(jnp.float32)

    def exchange(ref, sends, recvs, e, g, n):
        slot = (1 - e) * groups + member
        return pltpu.make_async_remote_copy(
            src_ref=ref.at[own], dst_ref=ref.at[slot], send_sem=sends.at[n], recv_sem=recvs.at[slot],
            device_id=place(e, g), device_id_type=MESH,
        )

    def arrival(ref, sends, recvs, e, g):
        slot = (1 + e) * groups + lax.rem(member + g, groups)
        return pltpu.make_async_remote_copy(
            src_ref=ref.at[own], dst_ref=ref.at[slot], send_sem=sends.at[0], recv_sem=recvs.at[slot],
            device_id=place(e, g), device_id_type=MESH,
        )

    pl.semaphore_wait(barrier, len(peers))
    first = [exchange(pool, send_sem, recv_sem, e, g, n) for n, (e, g) in enumerate(peers)]
    for copy in first:
        copy.start()
    for e, g in peers:
        arrival(pool, send_sem, recv_sem, e, g).wait_recv()

    def receiver(slot, cell):
        block = pool[slot, cell]
        rest = pool[slot, cells]
        length = rest[0:HALVES]
        for c in range(1, cells):
            length = jnp.where(cell == c, rest[c * HALVES:(c + 1) * HALVES], length)
        inverse = 1.0 / length
        rows = []
        for h in range(HALVES):
            rows.append([block[d * HALVES + h:d * HALVES + h + 1] for d in range(3)] + [inverse[h:h + 1]])
        return rows

    def chunks(source):
        for s in range(HALVES):
            for q in range(0, LANES, CHUNK):
                yield s, q, [source[q:q + CHUNK, d * HALVES + s:d * HALVES + s + 1] for d in range(4)]

    def inside(row, col):
        diffs = [row[d] - col[d] for d in range(3)]
        square = (diffs[0] * diffs[0] + diffs[1] * diffs[1] + diffs[2] * diffs[2]) * (row[3] * row[3])
        ratio = square * lax.rsqrt(jnp.maximum(square, 1e-30))
        return diffs, jnp.maximum(1.0 - ratio, 0.0)

    def task(t):
        recv, k = tasks_ref[0, t], tasks_ref[1, t]
        rows = receiver(groups + recv // cells, lax.rem(recv, cells))
        return rows, jnp.transpose(pool[k // cells, lax.rem(k, cells)])

    def density(t, carry):
        rows, source = task(t)
        total = [jnp.zeros((CHUNK, LANES), jnp.float32) for _ in range(HALVES)]
        for s, q, col in chunks(source):
            for h in range(HALVES):
                _, u = inside(rows[h], col)
                u2 = u * u
                total[h] = total[h] + (u2 * u2) * (5.0 - 4.0 * u) * col[3]
        for h in range(HALVES):
            value = jnp.sum(total[h], axis=0, keepdims=True)
            inv = rows[h][3]
            parts[own, pl.ds(t * HALVES + h, 1), :] = value * (inv * inv * inv) * DENSITY_SCALE
        return carry

    lax.fori_loop(0, pairs, density, 0)
    second = [exchange(parts, psend_sem, precv_sem, e, g, n) for n, (e, g) in enumerate(peers)]
    for copy in second:
        copy.start()

    def prepare(t, carry):
        rows, source = task(t)
        total = [[jnp.zeros((CHUNK, LANES), jnp.float32) for _ in range(3)] for _ in range(HALVES)]
        for s, q, col in chunks(source):
            for h in range(HALVES):
                diffs, u = inside(rows[h], col)
                coeff = (u * u) * u * col[3]
                for d in range(3):
                    term = coeff * diffs[d]
                    waiting[t, d * HALVES + h, pl.ds(s * LANES + q, CHUNK), :] = term
                    total[h][d] = total[h][d] + term
        for h in range(HALVES):
            inv = rows[h][3]
            early[t, pl.ds(3 * HALVES + h, 1), :] = FORCE_SCALE * (inv * inv) * (inv * inv) * inv
            for d in range(3):
                early[t, pl.ds(d * HALVES + h, 1), :] = jnp.sum(total[h][d], axis=0, keepdims=True)
        return carry

    lax.fori_loop(0, pairs, prepare, 0)

    for slot in range(3 * groups):
        for c in range(cells):
            m = pool[slot, c, pl.ds(3 * HALVES, HALVES), :]
            inv = 1.0 / pool[slot, cells, pl.ds(c * HALVES, HALVES), :]
            rho[pl.ds((slot * cells + c) * HALVES, HALVES), :] = m * (inv * inv * inv) * DENSITY_SCALE

    for e, g in peers:
        arrival(parts, psend_sem, precv_sem, e, g).wait_recv()

    span = slab_cells * HALVES
    index = lax.broadcasted_iota(jnp.int32, (span, LANES), 0)
    odd = lax.rem(index, HALVES)
    cell_of = (index // HALVES).astype(jnp.float32)
    for d in range(3):
        total = rho[pl.ds(d * span, span), :]
        for g in range(groups):
            slot = d * groups + g
            part = parts[slot]
            to = pool[slot, cells]
            for t in range(pairs):
                value = part[t * HALVES:t * HALVES + 1]
                for h in range(1, HALVES):
                    value = jnp.where(odd == h, part[t * HALVES + h:t * HALVES + h + 1], value)
                at = to[cells * HALVES + t:cells * HALVES + t + 1]
                total = total + jnp.where(cell_of == at, value, 0.0)
        rho[pl.ds(d * span, span), :] = total

    source_rho = [rho[pl.ds(tasks_ref[1, t] * HALVES, HALVES), :] for t in range(pairs)]
    source_rho = 1.0 / jnp.maximum(jnp.concatenate(source_rho, axis=0), 1e-30)
    columns = jnp.transpose(source_rho)
    for t in range(pairs):
        recv = tasks_ref[0, t]
        a_rho = 1.0 / jnp.maximum(rho[pl.ds((slab_cells + recv) * HALVES, HALVES), :], 1e-30)
        total = [[jnp.zeros((CHUNK, LANES), jnp.float32) for _ in range(3)] for _ in range(HALVES)]
        for s in range(HALVES):
            for q in range(0, LANES, CHUNK):
                col = columns[q:q + CHUNK, t * HALVES + s:t * HALVES + s + 1]
                for h in range(HALVES):
                    for d in range(3):
                        term = waiting[t, d * HALVES + h, pl.ds(s * LANES + q, CHUNK), :]
                        total[h][d] = total[h][d] + term * col
        for h in range(HALVES):
            for d in range(3):
                at = pl.ds(d * HALVES + h, 1)
                value = jnp.sum(total[h][d], axis=0, keepdims=True) + early[t, at, :] * a_rho[h:h + 1]
                forces[member, pl.ds((t * 3 + d) * HALVES + h, 1), :] = value * early[t, pl.ds(3 * HALVES + h, 1), :]

    third = []
    for g in range(1, groups):
        copy = pltpu.make_async_remote_copy(
            src_ref=forces.at[member], dst_ref=forces.at[member], send_sem=fsend_sem.at[g],
            recv_sem=frecv_sem.at[member], device_id=place(0, g), device_id_type=MESH,
        )
        copy.start()
        third.append(copy)

    live = []
    for c in range(cells):
        for h in range(HALVES):
            live.append((lane + h * LANES < counts_ref[c]).astype(jnp.float32))
            at = pl.ds(c * HALVES + h, 1)
            rho_out[at, :] = rho[pl.ds((own * cells + c) * HALVES + h, 1), :] * live[-1]

    for copy in first + second:
        copy.wait_send()
    for g in range(1, groups):
        other = lax.rem(member + g, groups)
        pltpu.make_async_remote_copy(
            src_ref=forces.at[member], dst_ref=forces.at[other], send_sem=fsend_sem.at[0],
            recv_sem=frecv_sem.at[other], device_id=place(0, g), device_id_type=MESH,
        ).wait_recv()

    rows = 3 * HALVES
    total = [jnp.zeros((rows, LANES), jnp.float32) for _ in range(cells)]
    base = (member * cells).astype(jnp.float32)
    for g in range(groups):
        to = pool[groups + g, cells]
        for t in range(pairs):
            value = forces[g, pl.ds(t * rows, rows), :]
            at = to[cells * HALVES + t:cells * HALVES + t + 1]
            for c in range(cells):
                total[c] = total[c] + jnp.where(at == base + c, value, 0.0)
    for c in range(cells):
        for h in range(HALVES):
            for d in range(3):
                row = total[c][d * HALVES + h:d * HALVES + h + 1] * live[c * HALVES + h]
                acc_out[pl.ds(d, 1), pl.ds(c * CELL + h * LANES, LANES)] = row

    for copy in third:
        copy.wait_send()


def local(positions, mass, smooth, counts, tasks):
    groups, doms = lax.axis_size("grp"), lax.axis_size("dom")
    cells, pairs = counts.shape[0], tasks.shape[1]
    around = 3 * groups
    last = max(8, -(-(cells * HALVES + pairs) // 8) * 8)
    vmem, hbm = (pl.BlockSpec(memory_space=space) for space in (pltpu.VMEM, pltpu.HBM))
    density, accel = pl.pallas_call(
        functools.partial(kernel, doms, groups, cells, pairs),
        out_shape=(
            jax.ShapeDtypeStruct((cells * HALVES, LANES), jnp.float32),
            jax.ShapeDtypeStruct(positions.shape, jnp.float32),
        ),
        in_specs=[hbm] * 5,
        out_specs=(vmem, vmem),
        scratch_shapes=[
            pltpu.SMEM(tasks.shape, jnp.int32),
            pltpu.SMEM(counts.shape, jnp.int32),
            pltpu.VMEM(positions.shape, jnp.float32),
            pltpu.VMEM((1, mass.shape[0]), jnp.float32),
            pltpu.VMEM((1, smooth.shape[0]), jnp.float32),
            pltpu.VMEM((around, cells + 1, last, LANES), jnp.float32),
            pltpu.VMEM((around, pairs * HALVES, LANES), jnp.float32),
            pltpu.VMEM((around * cells * HALVES, LANES), jnp.float32),
            pltpu.VMEM((groups, pairs * 3 * HALVES, LANES), jnp.float32),
            pltpu.VMEM((pairs, 3 * HALVES, CELL, LANES), jnp.float32),
            pltpu.VMEM((pairs, 4 * HALVES, LANES), jnp.float32),
            pltpu.SemaphoreType.DMA((5,)),
            pltpu.SemaphoreType.DMA((around,)),
            pltpu.SemaphoreType.DMA((around,)),
            pltpu.SemaphoreType.DMA((around,)),
            pltpu.SemaphoreType.DMA((around,)),
            pltpu.SemaphoreType.DMA((groups,)),
            pltpu.SemaphoreType.DMA((groups,)),
        ],
        compiler_params=pltpu.CompilerParams(
            collective_id=0, has_side_effects=True, vmem_limit_bytes=48 * 1024 * 1024
        ),
    )(tasks, counts, positions, mass[None], smooth[None])
    return density.reshape(-1), accel


def solution(mesh):
    in_specs = (
        P(None, ("dom", "grp")),
        P(("dom", "grp")),
        P(("dom", "grp")),
        P(("dom", "grp")),
        P(None, ("dom", "grp")),
    )
    out_specs = (P(("dom", "grp")), P(None, ("dom", "grp")))
    return jax.shard_map(local, mesh=mesh, in_specs=in_specs, out_specs=out_specs, check_vma=False)
```

time: 30.1 us -> 25.3 us (0.84)
  Pallas kernels: 25.9 us -> 21.1 us
    pallas_call x1, Pallas kernels: 25.9 us -> 21.1 us  [local(): pl.pallas_call(functools.partial(kernel, doms, groups, cells, pairs), out...]
    reshape x1 -> x0, local copies, waits for them, and re-layouts: 0.61 us -> none  [local(): return (density.reshape(-1), accel.reshape(3, -1))]
    unnamed x11 -> x12, local copies, waits for them, and re-layouts: 2.63 us -> 3.23 us
where the time goes in v2:
time: 25.3 us; the launch traced here: 25 us
  Pallas kernels  21.1 us (83%)
  local copies, waits for them, and re-layouts  3.23 us (13%)
  between operations  0.67 us (3%)
    pallas_call x1, Pallas kernels, local(): pl.pallas_call(functools.partial(kernel, doms, groups, cells, pairs), out...  21.1 us
    unnamed x12, local copies, waits for them, and re-layouts  3.23 us

profile of v2, /device:TPU:0, one launch (start us, length us, event | category | flops | bytes accessed | tf_op | source)
XLA Modules:
  0.0 25.0 jit_solution(9502449612430506699)
XLA Ops:
  0.6 0.0 copy-start.1
  0.6 0.0 copy-start.3
  0.7 0.0 copy-start.4
  0.7 0.7 %copy-done.1 = f32[512]{0:T(512)S(1)} copy-done((f32[512]{0:T(512)S(1)}, f32[512]{0:T(512)}, u32[]{:S(2)}) %copy-start.1) | copy-done | bytes 2072
  1.3 0.0 copy-done.3
  1.3 0.0 copy-done.4
  1.3 0.0 copy-start
  1.3 0.7 %copy-done = f32[3,512]{1,0:T(4,128)S(1)} copy-done((f32[3,512]{1,0:T(4,128)S(1)}, f32[3,512]{1,0:T(4,128)}, u32[]{:S(2)}) %copy-start) | copy-done | bytes 6168
  2.0 0.0 copy-start.2
  2.0 0.7 %copy-done.2 = f32[512]{0:T(512)S(1)} copy-done((f32[512]{0:T(512)S(1)}, f32[512]{0:T(512)}, u32[]{:S(2)}) %copy-start.2) | copy-done | bytes 2072
  2.7 21.1 %shard_map.68 = (f32[4,128]{1,0:T(4,128)S(1)}, f32[3,512]{1,0:T(4,128)S(1)}) custom-call(s32[2,4]{1,0:T(2,128)S(1)} %copy-done.3, s32[2]{0:T(128)S(1)} %copy-done.4, f32[3,512]{1,0:T(4,128)S(1)} %copy-done, f32[1,512]{1,0:T(1,128)S(1)} %bitcast.3, f32[1,512]{1,0:T(1,128)S(1)} %bitcast.4), custom_call_target="tpu_custom_call" | custom-call | tf_op jit(solution)/shard_map/pallas_call | solution.py:247
  23.8 0.6 %copy.9 = f32[512]{0:T(512)} copy(f32[512]{0:T(512)S(1)} %bitcast.5) | data formatting | bytes 4096
  24.4 0.6 %copy.10 = f32[3,512]{1,0:T(4,128)} copy(f32[3,512]{1,0:T(4,128)S(1)} %get-tuple-element.9) | data formatting | bytes 12288
Async XLA Ops:
  0.6 0.7 %copy-start.1 = (f32[512]{0:T(512)S(1)}, f32[512]{0:T(512)}, u32[]{:S(2)}) copy-start(f32[512]{0:T(512)} %param.6) | copy-start | bytes 6148
  0.6 0.7 %copy-start.3 = (s32[2,4]{1,0:T(2,128)S(1)}, s32[2,4]{1,0:T(2,128)}, u32[]{:S(2)}) copy-start(s32[2,4]{1,0:T(2,128)} %tasks_hbm.1) | copy-start | bytes 100
  0.7 0.7 %copy-start.4 = (s32[2]{0:T(128)S(1)}, s32[2]{0:T(128)}, u32[]{:S(2)}) copy-start(s32[2]{0:T(128)} %counts_hbm.1) | copy-start | bytes 28
  1.3 0.7 %copy-start = (f32[3,512]{1,0:T(4,128)S(1)}, f32[3,512]{1,0:T(4,128)}, u32[]{:S(2)}) copy-start(f32[3,512]{1,0:T(4,128)} %pos_hbm.1) | copy-start | bytes 18436
  2.0 0.7 %copy-start.2 = (f32[512]{0:T(512)S(1)}, f32[512]{0:T(512)}, u32[]{:S(2)}) copy-start(f32[512]{0:T(512)} %param.7) | copy-start | bytes 6148

commit v3 on v2

--- a/solution.py
+++ b/solution.py
@@ -21,14 +21,16 @@
     doms, groups, cells, pairs, tasks_hbm, counts_hbm, pos_hbm, mass_hbm, smooth_hbm,
     rho_out, acc_out,
     tasks_ref, counts_ref, pos_ref, mass_ref, smooth_ref,
-    pool, parts, rho, forces, waiting, early,
-    in_sem, send_sem, recv_sem, psend_sem, precv_sem, fsend_sem, frecv_sem,
+    pool, slab_tail, far_tail, parts, rho, to_owner, forces, waiting, early,
+    in_sem, send_sem, recv_sem, tsend_sem, trecv_sem, psend_sem, precv_sem, fsend_sem, frecv_sem,
 ):
     slab_cells = groups * cells
     dom = lax.axis_index("dom")
     member = lax.axis_index("grp")
     own = groups + member
-    peers = [(e, g) for e in (0, -1, 1) for g in range(groups) if not (e == 0 and g == 0)]
+    near = [(0, g) for g in range(1, groups)]
+    far = [(e, g) for g in range(groups) for e in (-1, 1)]
+    peers = far + near
 
     def place(e, g):
         return (lax.rem(dom + e + doms, doms), lax.rem(member + g, groups))
@@ -54,9 +56,9 @@
             for d in range(3):
                 pool[own, c, pl.ds(d * HALVES + h, 1), :] = pos_ref[pl.ds(d, 1), at]
             pool[own, c, pl.ds(3 * HALVES + h, 1), :] = mass_ref[:, at] * live
-            pool[own, cells, pl.ds(c * HALVES + h, 1), :] = smooth_ref[:, at]
+            slab_tail[member, pl.ds(c * HALVES + h, 1), :] = smooth_ref[:, at]
     for t in range(pairs):
-        pool[own, cells, pl.ds(cells * HALVES + t, 1), :] = jnp.full((1, LANES), tasks_ref[0, t]).astype(jnp.float32)
+        slab_tail[member, pl.ds(cells * HALVES + t, 1), :] = jnp.full((1, LANES), tasks_ref[0, t]).astype(jnp.float32)
 
     def exchange(ref, sends, recvs, e, g, n):
         slot = (1 - e) * groups + member
@@ -74,14 +76,29 @@
 
     pl.semaphore_wait(barrier, len(peers))
     first = [exchange(pool, send_sem, recv_sem, e, g, n) for n, (e, g) in enumerate(peers)]
+
+    def tail_copy(e, g, n, sender):
+        slot = ((1 - e) if n > 0 else (1 + e)) * groups + sender
+        dst = slab_tail.at[sender] if e == 0 else far_tail.at[slot]
+        return pltpu.make_async_remote_copy(
+            src_ref=slab_tail.at[member], dst_ref=dst, send_sem=tsend_sem.at[n], recv_sem=trecv_sem.at[slot],
+            device_id=place(e, g), device_id_type=MESH,
+        )
+
+    first += [tail_copy(e, g, n + 1, member) for n, (e, g) in enumerate(near + far)]
     for copy in first:
         copy.start()
     for e, g in peers:
         arrival(pool, send_sem, recv_sem, e, g).wait_recv()
+    for e, g in near:
+        tail_copy(e, g, 0, lax.rem(member + g, groups)).wait_recv()
+
+    def tail_of(slot):
+        return slab_tail.at[slot - groups] if slot // groups == 1 else far_tail.at[slot]
 
     def receiver(slot, cell):
         block = pool[slot, cell]
-        rest = pool[slot, cells]
+        rest = slab_tail[slot - groups]
         length = rest[0:HALVES]
         for c in range(1, cells):
             length = jnp.where(cell == c, rest[c * HALVES:(c + 1) * HALVES], length)
@@ -146,10 +163,12 @@
 
     lax.fori_loop(0, pairs, prepare, 0)
 
+    for e, g in far:
+        tail_copy(e, g, 0, lax.rem(member + g, groups)).wait_recv()
     for slot in range(3 * groups):
         for c in range(cells):
             m = pool[slot, c, pl.ds(3 * HALVES, HALVES), :]
-            inv = 1.0 / pool[slot, cells, pl.ds(c * HALVES, HALVES), :]
+            inv = 1.0 / tail_of(slot)[pl.ds(c * HALVES, HALVES), :]
             rho[pl.ds((slot * cells + c) * HALVES, HALVES), :] = m * (inv * inv * inv) * DENSITY_SCALE
 
     for e, g in peers:
@@ -164,7 +183,7 @@
         for g in range(groups):
             slot = d * groups + g
             part = parts[slot]
-            to = pool[slot, cells]
+            to = tail_of(slot)[...]
             for t in range(pairs):
                 value = part[t * HALVES:t * HALVES + 1]
                 for h in range(1, HALVES):
@@ -176,6 +195,7 @@
     source_rho = [rho[pl.ds(tasks_ref[1, t] * HALVES, HALVES), :] for t in range(pairs)]
     source_rho = 1.0 / jnp.maximum(jnp.concatenate(source_rho, axis=0), 1e-30)
     columns = jnp.transpose(source_rho)
+    to_cell = [None] * slab_cells
     for t in range(pairs):
         recv = tasks_ref[0, t]
         a_rho = 1.0 / jnp.maximum(rho[pl.ds((slab_cells + recv) * HALVES, HALVES), :], 1e-30)
@@ -187,16 +207,24 @@
                     for d in range(3):
                         term = waiting[t, d * HALVES + h, pl.ds(s * LANES + q, CHUNK), :]
                         total[h][d] = total[h][d] + term * col
-        for h in range(HALVES):
-            for d in range(3):
+        sums = []
+        for d in range(3):
+            for h in range(HALVES):
                 at = pl.ds(d * HALVES + h, 1)
                 value = jnp.sum(total[h][d], axis=0, keepdims=True) + early[t, at, :] * a_rho[h:h + 1]
-                forces[member, pl.ds((t * 3 + d) * HALVES + h, 1), :] = value * early[t, pl.ds(3 * HALVES + h, 1), :]
-
+                sums.append(value * early[t, pl.ds(3 * HALVES + h, 1), :])
+        sums = jnp.concatenate(sums, axis=0)
+        for cell in range(slab_cells):
+            value = jnp.where(recv == cell, sums, 0.0)
+            to_cell[cell] = value if t == 0 else to_cell[cell] + value
+
+    rows = 3 * HALVES
+    for cell in range(slab_cells):
+        to_owner[cell // cells, pl.ds(cell % cells * rows, rows), :] = to_cell[cell]
     third = []
     for g in range(1, groups):
         copy = pltpu.make_async_remote_copy(
-            src_ref=forces.at[member], dst_ref=forces.at[member], send_sem=fsend_sem.at[g],
+            src_ref=to_owner.at[lax.rem(member + g, groups)], dst_ref=forces.at[member], send_sem=fsend_sem.at[g],
             recv_sem=frecv_sem.at[member], device_id=place(0, g), device_id_type=MESH,
         )
         copy.start()
@@ -214,28 +242,32 @@
     for g in range(1, groups):
         other = lax.rem(member + g, groups)
         pltpu.make_async_remote_copy(
-            src_ref=forces.at[member], dst_ref=forces.at[other], send_sem=fsend_sem.at[0],
+            src_ref=to_owner.at[member], dst_ref=forces.at[other], send_sem=fsend_sem.at[0],
             recv_sem=frecv_sem.at[other], device_id=place(0, g), device_id_type=MESH,
         ).wait_recv()
 
-    rows = 3 * HALVES
-    total = [jnp.zeros((rows, LANES), jnp.float32) for _ in range(cells)]
-    base = (member * cells).astype(jnp.float32)
-    for g in range(groups):
-        to = pool[groups + g, cells]
-        for t in range(pairs):
-            value = forces[g, pl.ds(t * rows, rows), :]
-            at = to[cells * HALVES + t:cells * HALVES + t + 1]
-            for c in range(cells):
-                total[c] = total[c] + jnp.where(at == base + c, value, 0.0)
+    total = to_owner[member]
+    for g in range(1, groups):
+        total = total + forces[lax.rem(member + g, groups)]
     for c in range(cells):
         for h in range(HALVES):
             for d in range(3):
-                row = total[c][d * HALVES + h:d * HALVES + h + 1] * live[c * HALVES + h]
-                acc_out[pl.ds(d, 1), pl.ds(c * CELL + h * LANES, LANES)] = row
+                at = (c * 3 + d) * HALVES + h
+                acc_out[pl.ds(d, 1), pl.ds(c * CELL + h * LANES, LANES)] = total[at:at + 1] * live[c * HALVES + h]
 
     for copy in third:
         copy.wait_send()
+
+
+def deliver(density_hbm, accel_hbm, density_out, accel_out, sems):
+    copies = [
+        pltpu.make_async_copy(density_hbm, density_out, sems.at[0]),
+        pltpu.make_async_copy(accel_hbm, accel_out, sems.at[1]),
+    ]
+    for copy in copies:
+        copy.start()
+    for copy in copies:
+        copy.wait()
 
 
 def local(positions, mass, smooth, counts, tasks):
@@ -258,13 +290,18 @@
             pltpu.VMEM(positions.shape, jnp.float32),
             pltpu.VMEM((1, mass.shape[0]), jnp.float32),
             pltpu.VMEM((1, smooth.shape[0]), jnp.float32),
-            pltpu.VMEM((around, cells + 1, last, LANES), jnp.float32),
+            pltpu.VMEM((around, cells, 4 * HALVES, LANES), jnp.float32),
+            pltpu.VMEM((groups, last, LANES), jnp.float32),
+            pltpu.VMEM((around, last, LANES), jnp.float32),
             pltpu.VMEM((around, pairs * HALVES, LANES), jnp.float32),
             pltpu.VMEM((around * cells * HALVES, LANES), jnp.float32),
-            pltpu.VMEM((groups, pairs * 3 * HALVES, LANES), jnp.float32),
+            pltpu.VMEM((groups, cells * 3 * HALVES, LANES), jnp.float32),
+            pltpu.VMEM((groups, cells * 3 * HALVES, LANES), jnp.float32),
             pltpu.VMEM((pairs, 3 * HALVES, CELL, LANES), jnp.float32),
             pltpu.VMEM((pairs, 4 * HALVES, LANES), jnp.float32),
             pltpu.SemaphoreType.DMA((5,)),
+            pltpu.SemaphoreType.DMA((around,)),
+            pltpu.SemaphoreType.DMA((around,)),
             pltpu.SemaphoreType.DMA((around,)),
             pltpu.SemaphoreType.DMA((around,)),
             pltpu.SemaphoreType.DMA((around,)),
@@ -273,10 +310,20 @@
             pltpu.SemaphoreType.DMA((groups,)),
         ],
         compiler_params=pltpu.CompilerParams(
-            collective_id=0, has_side_effects=True, vmem_limit_bytes=48 * 1024 * 1024
+            collective_id=0, has_side_effects=True, vmem_limit_bytes=64 * 1024 * 1024
         ),
     )(tasks, counts, positions, mass[None], smooth[None])
-    return density.reshape(-1), accel
+    return pl.pallas_call(
+        deliver,
+        out_shape=(
+            jax.ShapeDtypeStruct(mass.shape, jnp.float32),
+            jax.ShapeDtypeStruct(positions.shape, jnp.float32),
+        ),
+        in_specs=[hbm] * 2,
+        out_specs=(hbm, hbm),
+        scratch_shapes=[pltpu.SemaphoreType.DMA((2,))],
+        compiler_params=pltpu.CompilerParams(vmem_limit_bytes=64 * 1024 * 1024),
+    )(density.reshape(-1), accel)
 
 
 def solution(mesh):

time: 25.3 us -> 23.5 us (0.929)
  local copies, waits for them, and re-layouts: 3.23 us -> 0 us
  Pallas kernels: 21.1 us -> 22.7 us
    unnamed x12 -> x0, local copies, waits for them, and re-layouts: 3.23 us -> none
    pallas_call x0 -> x1, Pallas kernels: none -> 1.43 us  [local(): pl.pallas_call(deliver, out_shape=(jax.ShapeDtypeStruct(mass.shape, jnp.f...]
where the time goes in v3:
time: 23.5 us; the launch traced here: 23.3 us
  Pallas kernels  22.7 us (97%)
  between operations  0.64 us (3%)
    pallas_call x1, Pallas kernels, local(): pl.pallas_call(functools.partial(kernel, doms, groups, cells, pairs), out...  21.3 us
    pallas_call x1, Pallas kernels, local(): pl.pallas_call(deliver, out_shape=(jax.ShapeDtypeStruct(mass.shape, jnp.f...  1.43 us

profile of v3, /device:TPU:0, one launch (start us, length us, event | category | flops | bytes accessed | tf_op | source)
XLA Modules:
  0.0 23.3 jit_solution(5441677751924370399)
XLA Ops:
  0.6 21.3 %shard_map.68 = (f32[4,128]{1,0:T(4,128)}, f32[3,512]{1,0:T(4,128)}) custom-call(s32[2,4]{1,0:T(2,128)} %tasks_hbm.1, s32[2]{0:T(128)} %counts_hbm.1, f32[3,512]{1,0:T(4,128)} %pos_hbm.1, f32[1,512]{1,0:T(1,128)} %bitcast.3, f32[1,512]{1,0:T(1,128)} %bitcast.4), custom_call_target="tpu_custom_call" | custom-call | tf_op jit(solution)/shard_map/pallas_call | solution.py:279
  21.9 1.4 %shard_map.69 = (f32[512]{0:T(512)}, f32[3,512]{1,0:T(4,128)}) custom-call(f32[512]{0:T(512)} %bitcast.5, f32[3,512]{1,0:T(4,128)} %get-tuple-element.5.accel_hbm), custom_call_target="tpu_custom_call" | custom-call | tf_op jit(solution)/shard_map/pallas_call | solution.py:316

commit v4 on v3

--- a/solution.py
+++ b/solution.py
@@ -21,23 +21,54 @@
     doms, groups, cells, pairs, tasks_hbm, counts_hbm, pos_hbm, mass_hbm, smooth_hbm,
     rho_out, acc_out,
     tasks_ref, counts_ref, pos_ref, mass_ref, smooth_ref,
-    pool, slab_tail, far_tail, parts, rho, to_owner, forces, waiting, early,
-    in_sem, send_sem, recv_sem, tsend_sem, trecv_sem, psend_sem, precv_sem, fsend_sem, frecv_sem,
+    pool, tail, slab_tail, parts, rho, to_owner, forces, waiting, early,
+    in_sem, main_sem, near_sem, far_sem, parts_sem, force_sem,
 ):
     slab_cells = groups * cells
     dom = lax.axis_index("dom")
     member = lax.axis_index("grp")
     own = groups + member
-    near = [(0, g) for g in range(1, groups)]
-    far = [(e, g) for g in range(groups) for e in (-1, 1)]
-    peers = far + near
-
-    def place(e, g):
-        return (lax.rem(dom + e + doms, doms), lax.rem(member + g, groups))
+    around = 3 * groups
+
+    def place(e, z):
+        return (lax.rem(dom + e + doms, doms), z)
+
+    def each_far(act):
+        def step(i, carry):
+            act(2 * lax.div(i, groups) - 1, lax.rem(member + i, groups), i)
+            return carry
+
+        lax.fori_loop(0, 2 * groups, step, 0)
+
+    def each_near(act):
+        def step(g, carry):
+            act(0, lax.rem(member + g, groups), 2 * groups + g)
+            return carry
+
+        lax.fori_loop(1, groups, step, 0)
+
+    def each(act):
+        each_far(act)
+        each_near(act)
+
+    def start(ref, sems):
+        def copy(e, z, n):
+            slot = (1 - e) * groups + member
+            pltpu.make_async_remote_copy(
+                src_ref=ref.at[own], dst_ref=ref.at[slot], send_sem=sems.at[0], recv_sem=sems.at[1],
+                device_id=place(e, z), device_id_type=MESH,
+            ).start()
+
+        return copy
+
+    def whole(ref, sems, count):
+        return pltpu.make_async_remote_copy(
+            src_ref=ref.at[pl.ds(0, count)], dst_ref=ref.at[pl.ds(0, count)], send_sem=sems.at[0],
+            recv_sem=sems.at[1], device_id=place(0, lax.rem(member + 1, groups)), device_id_type=MESH,
+        )
 
     barrier = pltpu.get_barrier_semaphore()
-    for e, g in peers:
-        pl.semaphore_signal(barrier, inc=1, device_id=place(e, g), device_id_type=MESH)
+    each(lambda e, z, n: pl.semaphore_signal(barrier, inc=1, device_id=place(e, z), device_id_type=MESH))
     moves = (
         (tasks_hbm, tasks_ref), (counts_hbm, counts_ref), (pos_hbm, pos_ref), (mass_hbm, mass_ref),
         (smooth_hbm, smooth_ref),
@@ -56,52 +87,24 @@
             for d in range(3):
                 pool[own, c, pl.ds(d * HALVES + h, 1), :] = pos_ref[pl.ds(d, 1), at]
             pool[own, c, pl.ds(3 * HALVES + h, 1), :] = mass_ref[:, at] * live
-            slab_tail[member, pl.ds(c * HALVES + h, 1), :] = smooth_ref[:, at]
+            tail[own, pl.ds(c * HALVES + h, 1), :] = smooth_ref[:, at]
     for t in range(pairs):
-        slab_tail[member, pl.ds(cells * HALVES + t, 1), :] = jnp.full((1, LANES), tasks_ref[0, t]).astype(jnp.float32)
-
-    def exchange(ref, sends, recvs, e, g, n):
-        slot = (1 - e) * groups + member
-        return pltpu.make_async_remote_copy(
-            src_ref=ref.at[own], dst_ref=ref.at[slot], send_sem=sends.at[n], recv_sem=recvs.at[slot],
-            device_id=place(e, g), device_id_type=MESH,
-        )
-
-    def arrival(ref, sends, recvs, e, g):
-        slot = (1 + e) * groups + lax.rem(member + g, groups)
-        return pltpu.make_async_remote_copy(
-            src_ref=ref.at[own], dst_ref=ref.at[slot], send_sem=sends.at[0], recv_sem=recvs.at[slot],
-            device_id=place(e, g), device_id_type=MESH,
-        )
-
-    pl.semaphore_wait(barrier, len(peers))
-    first = [exchange(pool, send_sem, recv_sem, e, g, n) for n, (e, g) in enumerate(peers)]
-
-    def tail_copy(e, g, n, sender):
-        slot = ((1 - e) if n > 0 else (1 + e)) * groups + sender
-        dst = slab_tail.at[sender] if e == 0 else far_tail.at[slot]
-        return pltpu.make_async_remote_copy(
-            src_ref=slab_tail.at[member], dst_ref=dst, send_sem=tsend_sem.at[n], recv_sem=trecv_sem.at[slot],
-            device_id=place(e, g), device_id_type=MESH,
-        )
-
-    first += [tail_copy(e, g, n + 1, member) for n, (e, g) in enumerate(near + far)]
-    for copy in first:
-        copy.start()
-    for e, g in peers:
-        arrival(pool, send_sem, recv_sem, e, g).wait_recv()
-    for e, g in near:
-        tail_copy(e, g, 0, lax.rem(member + g, groups)).wait_recv()
-
-    def tail_of(slot):
-        return slab_tail.at[slot - groups] if slot // groups == 1 else far_tail.at[slot]
+        tail[own, pl.ds(cells * HALVES + t, 1), :] = jnp.full((1, LANES), tasks_ref[0, t]).astype(jnp.float32)
+
+    pl.semaphore_wait(barrier, around - 1)
+    each(start(pool, main_sem))
+    each_near(start(tail, near_sem))
+    each_far(start(tail, far_sem))
+    whole(pool, main_sem, around - 1).wait_recv()
+    whole(tail, near_sem, groups - 1).wait_recv()
+    slab_tail[...] = tail[pl.ds(groups, groups)]
 
     def receiver(slot, cell):
         block = pool[slot, cell]
-        rest = slab_tail[slot - groups]
-        length = rest[0:HALVES]
+        lengths = slab_tail[slot - groups]
+        length = lengths[0:HALVES]
         for c in range(1, cells):
-            length = jnp.where(cell == c, rest[c * HALVES:(c + 1) * HALVES], length)
+            length = jnp.where(cell == c, lengths[c * HALVES:(c + 1) * HALVES], length)
         inverse = 1.0 / length
         rows = []
         for h in range(HALVES):
@@ -139,9 +142,7 @@
         return carry
 
     lax.fori_loop(0, pairs, density, 0)
-    second = [exchange(parts, psend_sem, precv_sem, e, g, n) for n, (e, g) in enumerate(peers)]
-    for copy in second:
-        copy.start()
+    each(start(parts, parts_sem))
 
     def prepare(t, carry):
         rows, source = task(t)
@@ -163,16 +164,14 @@
 
     lax.fori_loop(0, pairs, prepare, 0)
 
-    for e, g in far:
-        tail_copy(e, g, 0, lax.rem(member + g, groups)).wait_recv()
+    whole(tail, far_sem, 2 * groups).wait_recv()
     for slot in range(3 * groups):
         for c in range(cells):
             m = pool[slot, c, pl.ds(3 * HALVES, HALVES), :]
-            inv = 1.0 / tail_of(slot)[pl.ds(c * HALVES, HALVES), :]
+            inv = 1.0 / tail[slot, pl.ds(c * HALVES, HALVES), :]
             rho[pl.ds((slot * cells + c) * HALVES, HALVES), :] = m * (inv * inv * inv) * DENSITY_SCALE
 
-    for e, g in peers:
-        arrival(parts, psend_sem, precv_sem, e, g).wait_recv()
+    whole(parts, parts_sem, around - 1).wait_recv()
 
     span = slab_cells * HALVES
     index = lax.broadcasted_iota(jnp.int32, (span, LANES), 0)
@@ -183,7 +182,7 @@
         for g in range(groups):
             slot = d * groups + g
             part = parts[slot]
-            to = tail_of(slot)[...]
+            to = tail[slot]
             for t in range(pairs):
                 value = part[t * HALVES:t * HALVES + 1]
                 for h in range(1, HALVES):
@@ -221,14 +220,14 @@
     rows = 3 * HALVES
     for cell in range(slab_cells):
         to_owner[cell // cells, pl.ds(cell % cells * rows, rows), :] = to_cell[cell]
-    third = []
-    for g in range(1, groups):
-        copy = pltpu.make_async_remote_copy(
-            src_ref=to_owner.at[lax.rem(member + g, groups)], dst_ref=forces.at[member], send_sem=fsend_sem.at[g],
-            recv_sem=frecv_sem.at[member], device_id=place(0, g), device_id_type=MESH,
-        )
-        copy.start()
-        third.append(copy)
+
+    def owner_copy(e, z, n):
+        pltpu.make_async_remote_copy(
+            src_ref=to_owner.at[z], dst_ref=forces.at[member], send_sem=force_sem.at[0], recv_sem=force_sem.at[1],
+            device_id=place(0, z), device_id_type=MESH,
+        ).start()
+
+    each_near(owner_copy)
 
     live = []
     for c in range(cells):
@@ -237,14 +236,11 @@
             at = pl.ds(c * HALVES + h, 1)
             rho_out[at, :] = rho[pl.ds((own * cells + c) * HALVES + h, 1), :] * live[-1]
 
-    for copy in first + second:
-        copy.wait_send()
-    for g in range(1, groups):
-        other = lax.rem(member + g, groups)
-        pltpu.make_async_remote_copy(
-            src_ref=to_owner.at[member], dst_ref=forces.at[other], send_sem=fsend_sem.at[0],
-            recv_sem=frecv_sem.at[other], device_id=place(0, g), device_id_type=MESH,
-        ).wait_recv()
+    whole(pool, main_sem, around - 1).wait_send()
+    whole(tail, near_sem, groups - 1).wait_send()
+    whole(tail, far_sem, 2 * groups).wait_send()
+    whole(parts, parts_sem, around - 1).wait_send()
+    whole(forces, force_sem, groups - 1).wait_recv()
 
     total = to_owner[member]
     for g in range(1, groups):
@@ -255,8 +251,7 @@
                 at = (c * 3 + d) * HALVES + h
                 acc_out[pl.ds(d, 1), pl.ds(c * CELL + h * LANES, LANES)] = total[at:at + 1] * live[c * HALVES + h]
 
-    for copy in third:
-        copy.wait_send()
+    whole(forces, force_sem, groups - 1).wait_send()
 
 
 def deliver(density_hbm, accel_hbm, density_out, accel_out, sems):
@@ -291,8 +286,8 @@
             pltpu.VMEM((1, mass.shape[0]), jnp.float32),
             pltpu.VMEM((1, smooth.shape[0]), jnp.float32),
             pltpu.VMEM((around, cells, 4 * HALVES, LANES), jnp.float32),
+            pltpu.VMEM((around, last, LANES), jnp.float32),
             pltpu.VMEM((groups, last, LANES), jnp.float32),
-            pltpu.VMEM((around, last, LANES), jnp.float32),
             pltpu.VMEM((around, pairs * HALVES, LANES), jnp.float32),
             pltpu.VMEM((around * cells * HALVES, LANES), jnp.float32),
             pltpu.VMEM((groups, cells * 3 * HALVES, LANES), jnp.float32),
@@ -300,14 +295,11 @@
             pltpu.VMEM((pairs, 3 * HALVES, CELL, LANES), jnp.float32),
             pltpu.VMEM((pairs, 4 * HALVES, LANES), jnp.float32),
             pltpu.SemaphoreType.DMA((5,)),
-            pltpu.SemaphoreType.DMA((around,)),
-            pltpu.SemaphoreType.DMA((around,)),
-            pltpu.SemaphoreType.DMA((around,)),
-            pltpu.SemaphoreType.DMA((around,)),
-            pltpu.SemaphoreType.DMA((around,)),
-            pltpu.SemaphoreType.DMA((around,)),
-            pltpu.SemaphoreType.DMA((groups,)),
-            pltpu.SemaphoreType.DMA((groups,)),
+            pltpu.SemaphoreType.DMA((2,)),
+            pltpu.SemaphoreType.DMA((2,)),
+            pltpu.SemaphoreType.DMA((2,)),
+            pltpu.SemaphoreType.DMA((2,)),
+            pltpu.SemaphoreType.DMA((2,)),
         ],
         compiler_params=pltpu.CompilerParams(
             collective_id=0, has_side_effects=True, vmem_limit_bytes=64 * 1024 * 1024

time: 23.5 us -> 22.9 us (0.974)
  Pallas kernels: 22.7 us -> 22.1 us
    pallas_call x1, Pallas kernels: 21.3 us -> 20.7 us  [local(): pl.pallas_call(functools.partial(kernel, doms, groups, cells, pairs), out...]
where the time goes in v4:
time: 22.9 us; the launch traced here: 22.7 us
  Pallas kernels  22.1 us (97%)
  between operations  0.64 us (3%)
    pallas_call x1, Pallas kernels, local(): pl.pallas_call(functools.partial(kernel, doms, groups, cells, pairs), out...  20.7 us
    pallas_call x1, Pallas kernels, local(): pl.pallas_call(deliver, out_shape=(jax.ShapeDtypeStruct(mass.shape, jnp.f...  1.43 us

profile of v4, /device:TPU:0, one launch (start us, length us, event | category | flops | bytes accessed | tf_op | source)
XLA Modules:
  0.0 22.7 jit_solution(883473879526812430)
XLA Ops:
  0.6 20.7 %shard_map.68 = (f32[4,128]{1,0:T(4,128)}, f32[3,512]{1,0:T(4,128)}) custom-call(s32[2,4]{1,0:T(2,128)} %tasks_hbm.1, s32[2]{0:T(128)} %counts_hbm.1, f32[3,512]{1,0:T(4,128)} %pos_hbm.1, f32[1,512]{1,0:T(1,128)} %bitcast.3, f32[1,512]{1,0:T(1,128)} %bitcast.4), custom_call_target="tpu_custom_call" | custom-call | tf_op jit(solution)/shard_map/pallas_call | solution.py:274
  21.3 1.4 %shard_map.69 = (f32[512]{0:T(512)}, f32[3,512]{1,0:T(4,128)}) custom-call(f32[512]{0:T(512)} %bitcast.5, f32[3,512]{1,0:T(4,128)} %get-tuple-element.5.accel_hbm), custom_call_target="tpu_custom_call" | custom-call | tf_op jit(solution)/shard_map/pallas_call | solution.py:308

commit v5 on v4

--- a/solution.py
+++ b/solution.py
@@ -21,7 +21,7 @@
     doms, groups, cells, pairs, tasks_hbm, counts_hbm, pos_hbm, mass_hbm, smooth_hbm,
     rho_out, acc_out,
     tasks_ref, counts_ref, pos_ref, mass_ref, smooth_ref,
-    pool, tail, slab_tail, parts, rho, to_owner, forces, waiting, early,
+    pool, tail, slab_tail, parts, rho, to_owner, forces, waiting, early, columns, over_rho,
     in_sem, main_sem, near_sem, far_sem, parts_sem, force_sem,
 ):
     slab_cells = groups * cells
@@ -111,10 +111,14 @@
             rows.append([block[d * HALVES + h:d * HALVES + h + 1] for d in range(3)] + [inverse[h:h + 1]])
         return rows
 
-    def chunks(source):
-        for s in range(HALVES):
-            for q in range(0, LANES, CHUNK):
-                yield s, q, [source[q:q + CHUNK, d * HALVES + s:d * HALVES + s + 1] for d in range(4)]
+    def chunks(step, init):
+        def some(i, carry):
+            block = columns[pl.ds(pl.multiple_of(i * CHUNK, CHUNK), CHUNK), :]
+            for s in range(HALVES):
+                carry = step(s, i, [block[:, d * HALVES + s:d * HALVES + s + 1] for d in range(4)], carry)
+            return carry
+
+        return lax.fori_loop(0, LANES // CHUNK, some, init)
 
     def inside(row, col):
         diffs = [row[d] - col[d] for d in range(3)]
@@ -125,16 +129,21 @@
     def task(t):
         recv, k = tasks_ref[0, t], tasks_ref[1, t]
         rows = receiver(groups + recv // cells, lax.rem(recv, cells))
-        return rows, jnp.transpose(pool[k // cells, lax.rem(k, cells)])
+        columns[...] = jnp.transpose(pool[k // cells, lax.rem(k, cells)])
+        return rows
 
     def density(t, carry):
-        rows, source = task(t)
-        total = [jnp.zeros((CHUNK, LANES), jnp.float32) for _ in range(HALVES)]
-        for s, q, col in chunks(source):
+        rows = task(t)
+
+        def step(s, i, col, total):
+            new = []
             for h in range(HALVES):
                 _, u = inside(rows[h], col)
                 u2 = u * u
-                total[h] = total[h] + (u2 * u2) * (5.0 - 4.0 * u) * col[3]
+                new.append(total[h] + (u2 * u2) * (5.0 - 4.0 * u) * col[3])
+            return tuple(new)
+
+        total = chunks(step, tuple(jnp.zeros((CHUNK, LANES), jnp.float32) for _ in range(HALVES)))
         for h in range(HALVES):
             value = jnp.sum(total[h], axis=0, keepdims=True)
             inv = rows[h][3]
@@ -145,21 +154,26 @@
     each(start(parts, parts_sem))
 
     def prepare(t, carry):
-        rows, source = task(t)
-        total = [[jnp.zeros((CHUNK, LANES), jnp.float32) for _ in range(3)] for _ in range(HALVES)]
-        for s, q, col in chunks(source):
+        rows = task(t)
+
+        def step(s, i, col, total):
+            new = []
             for h in range(HALVES):
                 diffs, u = inside(rows[h], col)
                 coeff = (u * u) * u * col[3]
                 for d in range(3):
                     term = coeff * diffs[d]
-                    waiting[t, d * HALVES + h, pl.ds(s * LANES + q, CHUNK), :] = term
-                    total[h][d] = total[h][d] + term
+                    at = pl.ds(pl.multiple_of(s * LANES + i * CHUNK, CHUNK), CHUNK)
+                    waiting[t, d * HALVES + h, at, :] = term
+                    new.append(total[h * 3 + d] + term)
+            return tuple(new)
+
+        total = chunks(step, tuple(jnp.zeros((CHUNK, LANES), jnp.float32) for _ in range(3 * HALVES)))
         for h in range(HALVES):
             inv = rows[h][3]
             early[t, pl.ds(3 * HALVES + h, 1), :] = FORCE_SCALE * (inv * inv) * (inv * inv) * inv
             for d in range(3):
-                early[t, pl.ds(d * HALVES + h, 1), :] = jnp.sum(total[h][d], axis=0, keepdims=True)
+                early[t, pl.ds(d * HALVES + h, 1), :] = jnp.sum(total[h * 3 + d], axis=0, keepdims=True)
         return carry
 
     lax.fori_loop(0, pairs, prepare, 0)
@@ -191,17 +205,19 @@
                 total = total + jnp.where(cell_of == at, value, 0.0)
         rho[pl.ds(d * span, span), :] = total
 
-    source_rho = [rho[pl.ds(tasks_ref[1, t] * HALVES, HALVES), :] for t in range(pairs)]
-    source_rho = 1.0 / jnp.maximum(jnp.concatenate(source_rho, axis=0), 1e-30)
-    columns = jnp.transpose(source_rho)
-    to_cell = [None] * slab_cells
     for t in range(pairs):
+        k_rho = 1.0 / jnp.maximum(rho[pl.ds(tasks_ref[1, t] * HALVES, HALVES), :], 1e-30)
+        over_rho[t] = jnp.transpose(jnp.concatenate([k_rho] * (8 // HALVES), axis=0))
+    to_owner[...] = jnp.zeros_like(to_owner)
+    rows = 3 * HALVES
+
+    def finish(t, carry):
         recv = tasks_ref[0, t]
         a_rho = 1.0 / jnp.maximum(rho[pl.ds((slab_cells + recv) * HALVES, HALVES), :], 1e-30)
         total = [[jnp.zeros((CHUNK, LANES), jnp.float32) for _ in range(3)] for _ in range(HALVES)]
         for s in range(HALVES):
             for q in range(0, LANES, CHUNK):
-                col = columns[q:q + CHUNK, t * HALVES + s:t * HALVES + s + 1]
+                col = over_rho[t, pl.ds(q, CHUNK), pl.ds(s, 1)]
                 for h in range(HALVES):
                     for d in range(3):
                         term = waiting[t, d * HALVES + h, pl.ds(s * LANES + q, CHUNK), :]
@@ -214,12 +230,11 @@
                 sums.append(value * early[t, pl.ds(3 * HALVES + h, 1), :])
         sums = jnp.concatenate(sums, axis=0)
         for cell in range(slab_cells):
-            value = jnp.where(recv == cell, sums, 0.0)
-            to_cell[cell] = value if t == 0 else to_cell[cell] + value
-
-    rows = 3 * HALVES
-    for cell in range(slab_cells):
-        to_owner[cell // cells, pl.ds(cell % cells * rows, rows), :] = to_cell[cell]
+            at = pl.ds(cell % cells * rows, rows)
+            to_owner[cell // cells, at, :] += jnp.where(recv == cell, sums, 0.0)
+        return carry
+
+    lax.fori_loop(0, pairs, finish, 0)
 
     def owner_copy(e, z, n):
         pltpu.make_async_remote_copy(
@@ -294,6 +309,8 @@
             pltpu.VMEM((groups, cells * 3 * HALVES, LANES), jnp.float32),
             pltpu.VMEM((pairs, 3 * HALVES, CELL, LANES), jnp.float32),
             pltpu.VMEM((pairs, 4 * HALVES, LANES), jnp.float32),
+            pltpu.VMEM((LANES, 4 * HALVES), jnp.float32),
+            pltpu.VMEM((pairs, LANES, 8), jnp.float32),
             pltpu.SemaphoreType.DMA((5,)),
             pltpu.SemaphoreType.DMA((2,)),
             pltpu.SemaphoreType.DMA((2,)),

time: 22.9 us -> 24 us (1.048)
  Pallas kernels: 22.1 us -> 23.2 us
    pallas_call x1, Pallas kernels: 20.7 us -> 21.8 us  [local(): pl.pallas_call(functools.partial(kernel, doms, groups, cells, pairs), out...]
where the time goes in v5:
time: 24 us; the launch traced here: 23.9 us
  Pallas kernels  23.2 us (97%)
  between operations  0.64 us (3%)
    pallas_call x1, Pallas kernels, local(): pl.pallas_call(functools.partial(kernel, doms, groups, cells, pairs), out...  21.8 us
    pallas_call x1, Pallas kernels, local(): pl.pallas_call(deliver, out_shape=(jax.ShapeDtypeStruct(mass.shape, jnp.f...  1.43 us

profile of v5, /device:TPU:0, one launch (start us, length us, event | category | flops | bytes accessed | tf_op | source)
XLA Modules:
  0.0 23.9 jit_solution(11326537182791289953)
XLA Ops:
  0.6 21.8 %shard_map.68 = (f32[4,128]{1,0:T(4,128)}, f32[3,512]{1,0:T(4,128)}) custom-call(s32[2,4]{1,0:T(2,128)} %tasks_hbm.1, s32[2]{0:T(128)} %counts_hbm.1, f32[3,512]{1,0:T(4,128)} %pos_hbm.1, f32[1,512]{1,0:T(1,128)} %bitcast.3, f32[1,512]{1,0:T(1,128)} %bitcast.4), custom_call_target="tpu_custom_call" | custom-call | tf_op jit(solution)/shard_map/pallas_call | solution.py:289
  22.4 1.4 %shard_map.69 = (f32[512]{0:T(512)}, f32[3,512]{1,0:T(4,128)}) custom-call(f32[512]{0:T(512)} %bitcast.5, f32[3,512]{1,0:T(4,128)} %get-tuple-element.5.accel_hbm), custom_call_target="tpu_custom_call" | custom-call | tf_op jit(solution)/shard_map/pallas_call | solution.py:325

commit v6 on v4

--- a/solution.py
+++ b/solution.py
@@ -19,9 +19,9 @@
 
 def kernel(
     doms, groups, cells, pairs, tasks_hbm, counts_hbm, pos_hbm, mass_hbm, smooth_hbm,
-    rho_out, acc_out,
+    rho_out, forces,
     tasks_ref, counts_ref, pos_ref, mass_ref, smooth_ref,
-    pool, tail, slab_tail, parts, rho, to_owner, forces, waiting, early,
+    pool, tail, slab_tail, parts, rho, to_owner, rho_own, weights, waiting, early,
     in_sem, main_sem, near_sem, far_sem, parts_sem, force_sem,
 ):
     slab_cells = groups * cells
@@ -108,7 +108,7 @@
         inverse = 1.0 / length
         rows = []
         for h in range(HALVES):
-            rows.append([block[d * HALVES + h:d * HALVES + h + 1] for d in range(3)] + [inverse[h:h + 1]])
+            rows.append([block[d * HALVES + h:d * HALVES + h + 1] for d in range(3)] + [inverse[h:h + 1], block[3 * HALVES + h:3 * HALVES + h + 1]])
         return rows
 
     def chunks(source):
@@ -120,28 +120,27 @@
         diffs = [row[d] - col[d] for d in range(3)]
         square = (diffs[0] * diffs[0] + diffs[1] * diffs[1] + diffs[2] * diffs[2]) * (row[3] * row[3])
         ratio = square * lax.rsqrt(jnp.maximum(square, 1e-30))
-        return diffs, jnp.maximum(1.0 - ratio, 0.0)
+        return jnp.maximum(1.0 - ratio, 0.0)
 
     def task(t):
         recv, k = tasks_ref[0, t], tasks_ref[1, t]
         rows = receiver(groups + recv // cells, lax.rem(recv, cells))
         return rows, jnp.transpose(pool[k // cells, lax.rem(k, cells)])
 
-    def density(t, carry):
+    for t in range(pairs):
         rows, source = task(t)
         total = [jnp.zeros((CHUNK, LANES), jnp.float32) for _ in range(HALVES)]
         for s, q, col in chunks(source):
             for h in range(HALVES):
-                _, u = inside(rows[h], col)
+                u = inside(rows[h], col)
                 u2 = u * u
-                total[h] = total[h] + (u2 * u2) * (5.0 - 4.0 * u) * col[3]
+                heavy = u2 * col[3]
+                weights[t, h, pl.ds(s * LANES + q, CHUNK), :] = heavy * u
+                total[h] = total[h] + (heavy * u2) * (1.25 - u)
         for h in range(HALVES):
             value = jnp.sum(total[h], axis=0, keepdims=True)
             inv = rows[h][3]
-            parts[own, pl.ds(t * HALVES + h, 1), :] = value * (inv * inv * inv) * DENSITY_SCALE
-        return carry
-
-    lax.fori_loop(0, pairs, density, 0)
+            parts[own, pl.ds(t * HALVES + h, 1), :] = value * (inv * inv * inv) * (4.0 * DENSITY_SCALE)
     each(start(parts, parts_sem))
 
     def prepare(t, carry):
@@ -149,15 +148,15 @@
         total = [[jnp.zeros((CHUNK, LANES), jnp.float32) for _ in range(3)] for _ in range(HALVES)]
         for s, q, col in chunks(source):
             for h in range(HALVES):
-                diffs, u = inside(rows[h], col)
-                coeff = (u * u) * u * col[3]
+                weight = weights[t, h, pl.ds(s * LANES + q, CHUNK), :]
                 for d in range(3):
-                    term = coeff * diffs[d]
+                    term = weight * (rows[h][d] - col[d])
                     waiting[t, d * HALVES + h, pl.ds(s * LANES + q, CHUNK), :] = term
                     total[h][d] = total[h][d] + term
         for h in range(HALVES):
             inv = rows[h][3]
-            early[t, pl.ds(3 * HALVES + h, 1), :] = FORCE_SCALE * (inv * inv) * (inv * inv) * inv
+            fifth = FORCE_SCALE * (inv * inv) * (inv * inv) * inv
+            early[t, pl.ds(3 * HALVES + h, 1), :] = jnp.where(rows[h][4] > 0.0, fifth, 0.0)
             for d in range(3):
                 early[t, pl.ds(d * HALVES + h, 1), :] = jnp.sum(total[h][d], axis=0, keepdims=True)
         return carry
@@ -229,39 +228,47 @@
 
     each_near(owner_copy)
 
-    live = []
     for c in range(cells):
         for h in range(HALVES):
-            live.append((lane + h * LANES < counts_ref[c]).astype(jnp.float32))
-            at = pl.ds(c * HALVES + h, 1)
-            rho_out[at, :] = rho[pl.ds((own * cells + c) * HALVES + h, 1), :] * live[-1]
+            live = (lane + h * LANES < counts_ref[c]).astype(jnp.float32)
+            rho_own[pl.ds(c * HALVES + h, 1), :] = rho[pl.ds((own * cells + c) * HALVES + h, 1), :] * live
+    outs = [
+        pltpu.make_async_copy(to_owner.at[member], forces.at[member], in_sem.at[0]),
+        pltpu.make_async_copy(rho_own, rho_out, in_sem.at[1]),
+    ]
+    for copy in outs:
+        copy.start()
 
     whole(pool, main_sem, around - 1).wait_send()
     whole(tail, near_sem, groups - 1).wait_send()
     whole(tail, far_sem, 2 * groups).wait_send()
     whole(parts, parts_sem, around - 1).wait_send()
+    for copy in outs:
+        copy.wait()
     whole(forces, force_sem, groups - 1).wait_recv()
-
-    total = to_owner[member]
-    for g in range(1, groups):
-        total = total + forces[lax.rem(member + g, groups)]
-    for c in range(cells):
-        for h in range(HALVES):
-            for d in range(3):
-                at = (c * 3 + d) * HALVES + h
-                acc_out[pl.ds(d, 1), pl.ds(c * CELL + h * LANES, LANES)] = total[at:at + 1] * live[c * HALVES + h]
-
-    whole(forces, force_sem, groups - 1).wait_send()
-
-
-def deliver(density_hbm, accel_hbm, density_out, accel_out, sems):
-    copies = [
-        pltpu.make_async_copy(density_hbm, density_out, sems.at[0]),
-        pltpu.make_async_copy(accel_hbm, accel_out, sems.at[1]),
+    whole(to_owner, force_sem, groups - 1).wait_send()
+
+
+def deliver(density_hbm, forces_hbm, density_out, accel_out, density, forces, accel, sems):
+    ins = [
+        pltpu.make_async_copy(density_hbm, density, sems.at[0]),
+        pltpu.make_async_copy(forces_hbm, forces, sems.at[1]),
     ]
-    for copy in copies:
+    for copy in ins:
         copy.start()
-    for copy in copies:
+    ins[0].wait()
+    outs = [pltpu.make_async_copy(density, density_out, sems.at[2])]
+    outs[0].start()
+    ins[1].wait()
+    total = forces[0]
+    for g in range(1, forces.shape[0]):
+        total = total + forces[g]
+    for at in range(total.shape[0]):
+        c, d, h = at // (3 * HALVES), at // HALVES % 3, at % HALVES
+        accel[pl.ds(d, 1), pl.ds(c * CELL + h * LANES, LANES)] = total[at:at + 1]
+    outs.append(pltpu.make_async_copy(accel, accel_out, sems.at[3]))
+    outs[1].start()
+    for copy in outs:
         copy.wait()
 
 
@@ -270,15 +277,15 @@
     cells, pairs = counts.shape[0], tasks.shape[1]
     around = 3 * groups
     last = max(8, -(-(cells * HALVES + pairs) // 8) * 8)
-    vmem, hbm = (pl.BlockSpec(memory_space=space) for space in (pltpu.VMEM, pltpu.HBM))
-    density, accel = pl.pallas_call(
+    hbm = pl.BlockSpec(memory_space=pltpu.HBM)
+    density, forces = pl.pallas_call(
         functools.partial(kernel, doms, groups, cells, pairs),
         out_shape=(
             jax.ShapeDtypeStruct((cells * HALVES, LANES), jnp.float32),
-            jax.ShapeDtypeStruct(positions.shape, jnp.float32),
+            jax.ShapeDtypeStruct((groups, cells * 3 * HALVES, LANES), jnp.float32),
         ),
         in_specs=[hbm] * 5,
-        out_specs=(vmem, vmem),
+        out_specs=(hbm, hbm),
         scratch_shapes=[
             pltpu.SMEM(tasks.shape, jnp.int32),
             pltpu.SMEM(counts.shape, jnp.int32),
@@ -291,7 +298,8 @@
             pltpu.VMEM((around, pairs * HALVES, LANES), jnp.float32),
             pltpu.VMEM((around * cells * HALVES, LANES), jnp.float32),
             pltpu.VMEM((groups, cells * 3 * HALVES, LANES), jnp.float32),
-            pltpu.VMEM((groups, cells * 3 * HALVES, LANES), jnp.float32),
+            pltpu.VMEM((cells * HALVES, LANES), jnp.float32),
+            pltpu.VMEM((pairs, HALVES, CELL, LANES), jnp.float32),
             pltpu.VMEM((pairs, 3 * HALVES, CELL, LANES), jnp.float32),
             pltpu.VMEM((pairs, 4 * HALVES, LANES), jnp.float32),
             pltpu.SemaphoreType.DMA((5,)),
@@ -313,9 +321,14 @@
         ),
         in_specs=[hbm] * 2,
         out_specs=(hbm, hbm),
-        scratch_shapes=[pltpu.SemaphoreType.DMA((2,))],
+        scratch_shapes=[
+            pltpu.VMEM(mass.shape, jnp.float32),
+            pltpu.VMEM(forces.shape, jnp.float32),
+            pltpu.VMEM(positions.shape, jnp.float32),
+            pltpu.SemaphoreType.DMA((4,)),
+        ],
         compiler_params=pltpu.CompilerParams(vmem_limit_bytes=64 * 1024 * 1024),
-    )(density.reshape(-1), accel)
+    )(density.reshape(-1), forces)
 
 
 def solution(mesh):

time: 22.9 us -> 21.9 us (0.956)
  Pallas kernels: 22.1 us -> 21.1 us
    pallas_call x1, Pallas kernels: 20.7 us -> 19.7 us  [local(): pl.pallas_call(functools.partial(kernel, doms, groups, cells, pairs), out...]
where the time goes in v6:
time: 21.9 us; the launch traced here: 21.7 us
  Pallas kernels  21.1 us (96%)
  between operations  0.64 us (3%)
    pallas_call x1, Pallas kernels, local(): pl.pallas_call(functools.partial(kernel, doms, groups, cells, pairs), out...  19.7 us
    pallas_call x1, Pallas kernels, local(): pl.pallas_call(deliver, out_shape=(jax.ShapeDtypeStruct(mass.shape, jnp.f...  1.38 us

profile of v6, /device:TPU:0, one launch (start us, length us, event | category | flops | bytes accessed | tf_op | source)
XLA Modules:
  0.0 21.7 jit_solution(11542928700740049826)
XLA Ops:
  0.6 19.7 %shard_map.68 = (f32[4,128]{1,0:T(4,128)}, f32[4,12,128]{2,1,0:T(8,128)}) custom-call(s32[2,4]{1,0:T(2,128)} %tasks_hbm.1, s32[2]{0:T(128)} %counts_hbm.1, f32[3,512]{1,0:T(4,128)} %pos_hbm.1, f32[1,512]{1,0:T(1,128)} %bitcast.3, f32[1,512]{1,0:T(1,128)} %bitcast.4), custom_call_target="tpu_custom_call" | custom-call | tf_op jit(solution)/shard_map/pallas_call | solution.py:281
  20.3 1.4 %shard_map.69 = (f32[512]{0:T(512)}, f32[3,512]{1,0:T(4,128)}) custom-call(f32[512]{0:T(512)} %bitcast.5, f32[4,12,128]{2,1,0:T(8,128)} %get-tuple-element.5.forces_hbm), custom_call_target="tpu_custom_call" | custom-call | tf_op jit(solution)/shard_map/pallas_call | solution.py:316

commit v7 on v6

--- a/solution.py
+++ b/solution.py
@@ -92,11 +92,11 @@
         tail[own, pl.ds(cells * HALVES + t, 1), :] = jnp.full((1, LANES), tasks_ref[0, t]).astype(jnp.float32)
 
     pl.semaphore_wait(barrier, around - 1)
+    each_near(start(tail, near_sem))
     each(start(pool, main_sem))
-    each_near(start(tail, near_sem))
-    each_far(start(tail, far_sem))
     whole(pool, main_sem, around - 1).wait_recv()
     whole(tail, near_sem, groups - 1).wait_recv()
+    each_far(start(tail, far_sem))
     slab_tail[...] = tail[pl.ds(groups, groups)]
 
     def receiver(slot, cell):

time: 21.9 us -> 21.9 us (level)
  no operation moved by 1% of the time
where the time goes in v7:
time: 21.9 us; the launch traced here: 21.6 us
  Pallas kernels  21 us (96%)
  between operations  0.64 us (3%)
    pallas_call x1, Pallas kernels, local(): pl.pallas_call(functools.partial(kernel, doms, groups, cells, pairs), out...  19.6 us
    pallas_call x1, Pallas kernels, local(): pl.pallas_call(deliver, out_shape=(jax.ShapeDtypeStruct(mass.shape, jnp.f...  1.38 us

profile of v7, /device:TPU:0, one launch (start us, length us, event | category | flops | bytes accessed | tf_op | source)
XLA Modules:
  0.0 21.6 jit_solution(14524562248840969847)
XLA Ops:
  0.6 19.6 %shard_map.68 = (f32[4,128]{1,0:T(4,128)}, f32[4,12,128]{2,1,0:T(8,128)}) custom-call(s32[2,4]{1,0:T(2,128)} %tasks_hbm.1, s32[2]{0:T(128)} %counts_hbm.1, f32[3,512]{1,0:T(4,128)} %pos_hbm.1, f32[1,512]{1,0:T(1,128)} %bitcast.3, f32[1,512]{1,0:T(1,128)} %bitcast.4), custom_call_target="tpu_custom_call" | custom-call | tf_op jit(solution)/shard_map/pallas_call | solution.py:281
  20.3 1.4 %shard_map.69 = (f32[512]{0:T(512)}, f32[3,512]{1,0:T(4,128)}) custom-call(f32[512]{0:T(512)} %bitcast.5, f32[4,12,128]{2,1,0:T(8,128)} %get-tuple-element.5.forces_hbm), custom_call_target="tpu_custom_call" | custom-call | tf_op jit(solution)/shard_map/pallas_call | solution.py:316

commit v8 on v7

--- a/solution.py
+++ b/solution.py
@@ -96,7 +96,6 @@
     each(start(pool, main_sem))
     whole(pool, main_sem, around - 1).wait_recv()
     whole(tail, near_sem, groups - 1).wait_recv()
-    each_far(start(tail, far_sem))
     slab_tail[...] = tail[pl.ds(groups, groups)]
 
     def receiver(slot, cell):
@@ -142,6 +141,7 @@
             inv = rows[h][3]
             parts[own, pl.ds(t * HALVES + h, 1), :] = value * (inv * inv * inv) * (4.0 * DENSITY_SCALE)
     each(start(parts, parts_sem))
+    each_far(start(tail, far_sem))
 
     def prepare(t, carry):
         rows, source = task(t)

time: 21.9 us -> 22.2 us (1.014)
  Pallas kernels: 21 us -> 21.4 us
    pallas_call x1, Pallas kernels: 19.6 us -> 20 us  [local(): pl.pallas_call(functools.partial(kernel, doms, groups, cells, pairs), out...]
where the time goes in v8:
time: 22.2 us; the launch traced here: 22 us
  Pallas kernels  21.4 us (96%)
  between operations  0.64 us (3%)
    pallas_call x1, Pallas kernels, local(): pl.pallas_call(functools.partial(kernel, doms, groups, cells, pairs), out...  20 us
    pallas_call x1, Pallas kernels, local(): pl.pallas_call(deliver, out_shape=(jax.ShapeDtypeStruct(mass.shape, jnp.f...  1.38 us

profile of v8, /device:TPU:0, one launch (start us, length us, event | category | flops | bytes accessed | tf_op | source)
XLA Modules:
  0.0 22.0 jit_solution(4218885944630252672)
XLA Ops:
  0.6 20.0 %shard_map.68 = (f32[4,128]{1,0:T(4,128)}, f32[4,12,128]{2,1,0:T(8,128)}) custom-call(s32[2,4]{1,0:T(2,128)} %tasks_hbm.1, s32[2]{0:T(128)} %counts_hbm.1, f32[3,512]{1,0:T(4,128)} %pos_hbm.1, f32[1,512]{1,0:T(1,128)} %bitcast.3, f32[1,512]{1,0:T(1,128)} %bitcast.4), custom_call_target="tpu_custom_call" | custom-call | tf_op jit(solution)/shard_map/pallas_call | solution.py:281
  20.6 1.4 %shard_map.69 = (f32[512]{0:T(512)}, f32[3,512]{1,0:T(4,128)}) custom-call(f32[512]{0:T(512)} %bitcast.5, f32[4,12,128]{2,1,0:T(8,128)} %get-tuple-element.5.forces_hbm), custom_call_target="tpu_custom_call" | custom-call | tf_op jit(solution)/shard_map/pallas_call | solution.py:316

commit v9 on v6

--- a/solution.py
+++ b/solution.py
@@ -11,7 +11,7 @@
 CELL = 256
 LANES = 128
 HALVES = CELL // LANES
-CHUNK = 32
+CHUNK = 16
 MESH = pl.DeviceIdType.MESH
 DENSITY_SCALE = 21.0 / (2.0 * math.pi)
 FORCE_SCALE = 105.0 / math.pi

time: 21.9 us -> 21.9 us (level)
  no operation moved by 1% of the time
where the time goes in v9:
time: 21.9 us; the launch traced here: 21.7 us
  Pallas kernels  21.1 us (96%)
  between operations  0.64 us (3%)
    pallas_call x1, Pallas kernels, local(): pl.pallas_call(functools.partial(kernel, doms, groups, cells, pairs), out...  19.7 us
    pallas_call x1, Pallas kernels, local(): pl.pallas_call(deliver, out_shape=(jax.ShapeDtypeStruct(mass.shape, jnp.f...  1.38 us

profile of v9, /device:TPU:0, one launch (start us, length us, event | category | flops | bytes accessed | tf_op | source)
XLA Modules:
  0.0 21.7 jit_solution(13137741746819586867)
XLA Ops:
  0.6 19.7 %shard_map.68 = (f32[4,128]{1,0:T(4,128)}, f32[4,12,128]{2,1,0:T(8,128)}) custom-call(s32[2,4]{1,0:T(2,128)} %tasks_hbm.1, s32[2]{0:T(128)} %counts_hbm.1, f32[3,512]{1,0:T(4,128)} %pos_hbm.1, f32[1,512]{1,0:T(1,128)} %bitcast.3, f32[1,512]{1,0:T(1,128)} %bitcast.4), custom_call_target="tpu_custom_call" | custom-call | tf_op jit(solution)/shard_map/pallas_call | solution.py:281
  20.3 1.4 %shard_map.69 = (f32[512]{0:T(512)}, f32[3,512]{1,0:T(4,128)}) custom-call(f32[512]{0:T(512)} %bitcast.5, f32[4,12,128]{2,1,0:T(8,128)} %get-tuple-element.5.forces_hbm), custom_call_target="tpu_custom_call" | custom-call | tf_op jit(solution)/shard_map/pallas_call | solution.py:316

commit v10 on v6

--- a/solution.py
+++ b/solution.py
@@ -35,7 +35,7 @@
 
     def each_far(act):
         def step(i, carry):
-            act(2 * lax.div(i, groups) - 1, lax.rem(member + i, groups), i)
+            act(2 * lax.rem(i, 2) - 1, lax.rem(member + 1 + lax.div(i, 2), groups), i)
             return carry
 
         lax.fori_loop(0, 2 * groups, step, 0)

time: 21.9 us -> 22 us (level)
  no operation moved by 1% of the time
where the time goes in v10:
time: 22 us; the launch traced here: 21.8 us
  Pallas kernels  21.1 us (96%)
  between operations  0.64 us (3%)
    pallas_call x1, Pallas kernels, local(): pl.pallas_call(functools.partial(kernel, doms, groups, cells, pairs), out...  19.7 us
    pallas_call x1, Pallas kernels, local(): pl.pallas_call(deliver, out_shape=(jax.ShapeDtypeStruct(mass.shape, jnp.f...  1.38 us

profile of v10, /device:TPU:0, one launch (start us, length us, event | category | flops | bytes accessed | tf_op | source)
XLA Modules:
  0.0 21.8 jit_solution(15354856679181468142)
XLA Ops:
  0.6 19.7 %shard_map.68 = (f32[4,128]{1,0:T(4,128)}, f32[4,12,128]{2,1,0:T(8,128)}) custom-call(s32[2,4]{1,0:T(2,128)} %tasks_hbm.1, s32[2]{0:T(128)} %counts_hbm.1, f32[3,512]{1,0:T(4,128)} %pos_hbm.1, f32[1,512]{1,0:T(1,128)} %bitcast.3, f32[1,512]{1,0:T(1,128)} %bitcast.4), custom_call_target="tpu_custom_call" | custom-call | tf_op jit(solution)/shard_map/pallas_call | solution.py:281
  20.4 1.4 %shard_map.69 = (f32[512]{0:T(512)}, f32[3,512]{1,0:T(4,128)}) custom-call(f32[512]{0:T(512)} %bitcast.5, f32[4,12,128]{2,1,0:T(8,128)} %get-tuple-element.5.forces_hbm), custom_call_target="tpu_custom_call" | custom-call | tf_op jit(solution)/shard_map/pallas_call | solution.py:316
